TPU v7x, 32 devices: a whole 2x2x4 slice. The times are simulated.
32 devices in a mesh: blk: 8 (over z, y), nbr: 4 (over x, core).
Axes of the slice: x: 2, y: 2, z: 4, core: 2. Of those that a mesh axis runs over, the one named last changes fastest.
Arguments:
- positions: float32 [3, 16384], P(None, ('blk', 'nbr')), may hold values from -6 to 6
- density: float32 [3, 16384], P(None, ('blk', 'nbr')), may hold values from -1.2 to 1.2
- upsample: float32 [32, 128], replicated, may hold values from -1 to 1
- cell_map: int32 [8, 4], P('blk'), may hold values from 0 to 3, as said below
- near_list: int32 [32, 12, 2], P(('blk', 'nbr')), may hold values from -1 to 15, as said below
Outputs:
- velocity: float32 [3, 16384], P(None, ('blk', 'nbr'))
Inputs may be any that keep to these rules, and one draw needn't show every extreme that they name: Each row of cell_map is a permutation of the nbr indices. In near_list[c] every entry is either (-1, -1) or a pair (k, t) with t a cell id of c's row other than c's own; the pairs of one list are distinct; no cell id is named by more than 4 entries of one list, and in every row one cell is named by exactly 4 entries of every other cell's list.
All inputs are finite; a program needn't handle non-finite values.
Results may differ from a plain program's by a relative error of at most 0.0003.
Values sent between devices are 32-bit elements; how exact they have to be, the bound alone decides.
No kernel may reach another device: no remote copies, remote signals or barrier semaphores. Data moves between devices by JAX's collectives and lax.ppermute only.
A program may use at most 64 MiB of HBM per device.

v0:
```python
import functools
import math

import jax
import jax.numpy as jnp
from jax import lax
from jax.experimental import pallas as pl
from jax.experimental.pallas import tpu as pltpu
from jax.sharding import PartitionSpec as P

FAR_REG_SQ = 0.0625
NEAR_REG_SQ = 0.01
STOKES_COEF = 1.0 / (8.0 * math.pi)
F32 = jnp.float32
BF16 = jnp.bfloat16
LANES = 128
ROWS = 8
VMEM_LIMIT = 40 * 2**20


def split3(a):
    hi = a.astype(BF16).astype(F32)
    rest = a - hi
    mid = rest.astype(BF16).astype(F32)
    return hi, mid, rest - mid


def split2(a):
    hi = a.astype(BF16)
    return hi, (a - hi.astype(F32)).astype(BF16)


def stack_left(a):
    hi, mid, lo = split3(a)
    return jnp.concatenate([hi, hi, mid, mid, hi, lo], axis=0).astype(BF16)


def stack_right(a):
    hi, mid, lo = split3(a)
    return jnp.concatenate([hi, mid, hi, mid, lo, hi], axis=0).astype(BF16)


def stack_two(a):
    hi = a.astype(BF16).astype(F32)
    return jnp.concatenate([hi, a - hi], axis=0).astype(BF16)


def pad_rows(parts):
    have = sum(p.shape[0] for p in parts)
    return jnp.concatenate(parts + [jnp.zeros((ROWS - have, parts[0].shape[1]), F32)], axis=0)


def dot_first(a, b):
    return lax.dot_general(a, b, (((0,), (0,)), ((), ())), preferred_element_type=F32)


def dot(a, b):
    return jnp.dot(a, b, preferred_element_type=F32)


def target_features(x, reg_sq):
    inv = 1.0 / reg_sq
    ones = jnp.ones((1, x.shape[1]), F32)
    norm = jnp.sum(x * x, axis=0, keepdims=True) * inv
    dist = stack_right(pad_rows([(-2.0 * inv) * x, ones, norm]))
    return dist


def project_features(x):
    return stack_right(pad_rows([x, jnp.ones((1, x.shape[1]), F32)]))


def block_sum(source, dist_t, proj_t, reg_sq):
    inv = 1.0 / reg_sq
    inv_len = 1.0 / math.sqrt(reg_sq)
    y = source[0:3]
    f = source[3:6]
    ones = jnp.ones((1, y.shape[1]), F32)
    norm = jnp.sum(y * y, axis=0, keepdims=True) * inv + 1.0
    along = jnp.sum(y * f, axis=0, keepdims=True)
    dist_s = stack_left(pad_rows([y, norm, ones]))
    proj_s = stack_left(pad_rows([f, -along]))
    first = stack_two(pad_rows([f * inv_len]))
    second = stack_two(pad_rows([-y, ones]) * inv_len**3)
    root = lax.rsqrt(dot_first(dist_s, dist_t))
    cube = root * root * root
    lead_hi, lead_lo = split2(root + cube)
    q_hi, q_lo = split2(dot_first(proj_s, proj_t) * cube)
    return (dot(first, lead_hi) + dot(first, lead_lo)) + (dot(second, q_hi) + dot(second, q_lo))


def upsample_tiles(tiles, table):
    panel_pts, fine_pts = table.shape
    group = LANES // panel_pts
    zero = jnp.zeros((panel_pts, fine_pts), F32)
    spread = jnp.concatenate(
        [jnp.concatenate([table if h == g else zero for h in range(group)], axis=1) for g in range(group)], axis=0
    )
    t_hi, t_mid, t_lo = split3(jnp.concatenate(tiles, axis=0))
    w_hi, w_mid, w_lo = (w.astype(BF16) for w in split3(spread))
    n = t_hi.shape[0]
    on_hi = dot(jnp.concatenate([t_hi, t_mid, t_lo], axis=0).astype(BF16), w_hi)
    on_mid = dot(jnp.concatenate([t_hi, t_mid], axis=0).astype(BF16), w_mid)
    on_lo = dot(t_hi.astype(BF16), w_lo)
    fine = on_hi[0:n] + (on_hi[n : 2 * n] + on_mid[0:n]) + (on_hi[2 * n :] + on_mid[n:] + on_lo)
    ratio = panel_pts / fine_pts
    scale = jnp.where(lax.broadcasted_iota(jnp.int32, fine.shape, 0) % ROWS < 3, 1.0, ratio)
    fine = fine * scale
    return [fine[ROWS * i : ROWS * (i + 1)] for i in range(len(tiles))]


def pack_kernel(peers, slots, entries, panel_pts, pos_ref, den_ref, list_ref, map_ref, own_ref, *rest):
    tile_refs = rest[: peers - 1]
    table, count = rest[peers - 1 :]
    own_ref[0:3, :] = pos_ref[...]
    own_ref[3:6, :] = den_ref[...]
    own_ref[6:8, :] = jnp.zeros((2, own_ref.shape[1]), F32)
    me = lax.axis_index("nbr")

    def clear(i, _):
        table[i] = -1
        return 0

    lax.fori_loop(0, peers * slots + 1, clear, 0, unroll=True)
    for i in range(peers + 1):
        count[i] = 0

    def place(e, _):
        panel = list_ref[e, 0]
        cell = list_ref[e, 1]
        valid = cell >= 0
        dest = map_ref[0, jnp.maximum(cell, 0)]
        at = jnp.where(valid, dest, peers)
        rank = count[at]
        count[at] = rank + 1
        table[jnp.where(valid, dest * slots + rank, peers * slots)] = panel
        return 0

    lax.fori_loop(0, entries, place, 0, unroll=entries <= 16)
    group = LANES // panel_pts
    lane_group = lax.broadcasted_iota(jnp.int32, (ROWS, LANES), 1) // panel_pts
    for d in range(1, peers):
        dest = me ^ d
        tile = jnp.zeros((ROWS, LANES), F32)
        for s in range(slots):
            panel = table[dest * slots + s]
            safe = jnp.maximum(panel, 0)
            start = pl.multiple_of((safe // group) * LANES, LANES)
            piece = own_ref[:, pl.ds(start, LANES)]
            shift = (s - safe % group + group) % group * panel_pts
            moved = pltpu.roll(piece, shift, 1)
            tile = jnp.where((lane_group == s) & (panel >= 0), moved, tile)
        tile_refs[d - 1][...] = tile


def pack(positions, density, near_list, cell_map, panel_pts, peers):
    points = positions.shape[1]
    entries = near_list.shape[0]
    slots = LANES // panel_pts
    vmem = pl.BlockSpec(memory_space=pltpu.VMEM)
    smem = pl.BlockSpec(memory_space=pltpu.SMEM)
    return pl.pallas_call(
        functools.partial(pack_kernel, peers, slots, entries, panel_pts),
        out_shape=[jax.ShapeDtypeStruct((ROWS, points), F32)]
        + [jax.ShapeDtypeStruct((ROWS, LANES), F32)] * (peers - 1),
        in_specs=[vmem, vmem, smem, smem],
        out_specs=[vmem] * peers,
        scratch_shapes=[pltpu.SMEM((peers * slots + 1,), jnp.int32), pltpu.SMEM((peers + 1,), jnp.int32)],
        compiler_params=pltpu.CompilerParams(vmem_limit_bytes=VMEM_LIMIT),
        name="pack",
    )(positions, density, near_list, cell_map)


def sum_kernel(n_far, n_near, has_prior, final, *refs):
    refs = list(refs)
    x_ref = refs.pop(0)
    prior = refs.pop(0)[...] if has_prior else None
    far_refs = [refs.pop(0) for _ in range(n_far)]
    near_refs = [refs.pop(0) for _ in range(n_near)]
    table_ref = refs.pop(0) if n_near else None
    out_ref = refs.pop(0)
    x = x_ref[0:3, :]
    proj_t = project_features(x)
    total = jnp.zeros((2 * ROWS, x.shape[1]), F32)
    if n_far:
        dist_t = target_features(x, FAR_REG_SQ)
        for ref in far_refs:
            if len(ref.shape) == 2:
                total = total + block_sum(ref[...], dist_t, proj_t, FAR_REG_SQ)
            elif ref.shape[0] <= 4:
                for i in range(ref.shape[0]):
                    total = total + block_sum(ref[i], dist_t, proj_t, FAR_REG_SQ)
            else:
                total = lax.fori_loop(
                    0, ref.shape[0], lambda i, t, ref=ref: t + block_sum(ref[i], dist_t, proj_t, FAR_REG_SQ), total
                )
    if n_near:
        dist_t = target_features(x, NEAR_REG_SQ)
        for start in range(0, n_near, 3):
            for fine in upsample_tiles([r[...] for r in near_refs[start : start + 3]], table_ref[...]):
                total = total + block_sum(fine, dist_t, proj_t, NEAR_REG_SQ)
    summed = total[0:ROWS] + total[ROWS:]
    if has_prior:
        summed = summed + prior
    if final:
        out_ref[...] = STOKES_COEF * (summed[0:3] + x * summed[3:4])
    else:
        out_ref[...] = summed


def pair_sums(name, own, prior, far, near, table, final):
    points = own.shape[1]
    vmem = pl.BlockSpec(memory_space=pltpu.VMEM)
    args = [own] + ([prior] if prior is not None else []) + list(far) + list(near) + ([table] if near else [])
    pairs = points * (
        sum(a.size // ROWS for a in far) + (sum(a.size // ROWS for a in near) * table.shape[1] // table.shape[0] if near else 0)
    )
    return pl.pallas_call(
        functools.partial(sum_kernel, len(far), len(near), prior is not None, final),
        out_shape=jax.ShapeDtypeStruct((3 if final else ROWS, points), F32),
        in_specs=[vmem] * len(args),
        out_specs=vmem,
        compiler_params=pltpu.CompilerParams(vmem_limit_bytes=VMEM_LIMIT),
        cost_estimate=pl.CostEstimate(flops=300 * pairs, bytes_accessed=0, transcendentals=pairs),
        name=name,
    )(*args)


def flips(size, bit):
    return [(i, i ^ bit) for i in range(size)]


MODE = "B"


def shards(positions, density, upsample, cell_map, near_list):
    columns = lax.axis_size("blk")
    peers = lax.axis_size("nbr")
    own, *tiles = pack(positions, density, near_list[0], cell_map, upsample.shape[0], peers)
    if MODE == "B":
        bits = [b for b in (2, 4, 6) if b < columns]
        zs = [lax.ppermute(own, "blk", flips(columns, b)) for b in (6, 4, 2)]
        near = [lax.ppermute(t, "nbr", flips(peers, d + 1)) for d, t in enumerate(tiles)]
        part = pair_sums("own_far", own, None, [own], [], upsample, False)
        part = pair_sums("near", own, part, [], near, upsample, False)
        four = jnp.stack([own] + zs)
        other = lax.ppermute(four, "blk", flips(columns, 1))
        part = pair_sums("far_z", own, part, zs, [], upsample, False)
        rest = [other]
        bit = 8
        while bit < columns:
            both = jnp.concatenate([four, other]) if bit == 8 else jnp.concatenate([both, more])
            more = lax.ppermute(both, "blk", flips(columns, bit))
            rest.append(more)
            bit *= 2
        return pair_sums("far_y", own, part, rest, [], upsample, True)


def solution(mesh):
    placed = (
        P(None, ("blk", "nbr")),
        P(None, ("blk", "nbr")),
        P(),
        P("blk", None),
        P(("blk", "nbr"), None, None),
    )
    return jax.shard_map(
        shards, mesh=mesh, in_specs=placed, out_specs=P(None, ("blk", "nbr")), check_vma=False
    )
```

profile of v0, /device:TPU:0, one launch (start us, length us, event | category | flops | bytes accessed | tf_op | source)
XLA Modules:
  0.0 28.8 jit_solution(3462863827165270036)
XLA Ops:
  0.0 0.7 %copy-done.4 = s32[1,12,2]{1,2,0:T(2,128)S(1)} copy-done((s32[1,12,2]{1,2,0:T(2,128)S(1)}, s32[1,12,2]{1,2,0:T(2,128)}, u32[]{:S(2)}) %copy-start.4) | copy-done | bytes 120
  0.7 0.1 copy.6.list_ref
  0.8 0.0 copy-done
  0.8 0.6 %copy-done.2 = s32[1,4]{1,0:T(1,128)S(1)} copy-done((s32[1,4]{1,0:T(1,128)S(1)}, s32[1,4]{1,0:T(1,128)}, u32[]{:S(2)}) %copy-start.2) | copy-done | bytes 40
  1.3 0.7 %copy-done.1 = f32[3,512]{1,0:T(4,128)S(1)} copy-done((f32[3,512]{1,0:T(4,128)S(1)}, f32[3,512]{1,0:T(4,128)}, u32[]{:S(2)}) %copy-start.1) | copy-done | bytes 6168
  2.0 0.9 %pack.1 = (f32[8,512]{1,0:T(8,128)S(1)}, f32[8,128]{1,0:T(8,128)S(1)}, f32[8,128]{1,0:T(8,128)S(1)}, f32[8,128]{1,0:T(8,128)S(1)}) custom-call(f32[3,512]{1,0:T(4,128)S(1)} %copy-done, f32[3,512]{1,0:T(4,128)S(1)} %copy-done.1, s32[12,2]{1,0:T(8,128)S(1)} %copy.6.list_ref, s32[1,4]{1,0:T(1,128)S(1)} %copy-done.2), custom_call_target="tpu_custom_call" | custom-call | tf_op jit(solution)/shard_map/pack/pallas_call | solution.py:162
  2.9 3.1 %collective-permute-start.5 = (f32[8,512]{1,0:T(8,128)S(1)}, f32[8,512]{1,0:T(8,128)S(1)}, u32[]{:S(2)}, u32[]{:S(2)}) collective-permute-start(f32[8,512]{1,0:T(8,128)S(1)} %get-tuple-element.9.refs_0_.refs_1_), channel_id=1, source_target_pairs={{0,8},{4,12},{8,0},{12,4},{16,24},{20,28},{24,16},{28,20},{1,9},{5... | collective-permute-start | bytes 49160 | tf_op jit(solution)/shard_map/ppermute | solution.py:242
  6.0 2.6 %collective-permute-start.4 = (f32[8,512]{1,0:T(8,128)S(1)}, f32[8,512]{1,0:T(8,128)S(1)}, u32[]{:S(2)}, u32[]{:S(2)}) collective-permute-start(f32[8,512]{1,0:T(8,128)S(1)} %get-tuple-element.9.refs_0_.refs_1_), channel_id=1, source_target_pairs={{0,16},{4,20},{8,24},{12,28},{16,0},{20,4},{24,8},{28,12},{1,17},{... | collective-permute-start | bytes 49160 | tf_op jit(solution)/shard_map/ppermute | solution.py:242
  8.6 0.0 collective-permute-start.3
  8.6 0.0 collective-permute-done.5.refs_4_
  8.6 2.1 %collective-permute-done.4.refs_3_ = f32[8,512]{1,0:T(8,128)S(1)} collective-permute-done((f32[8,512]{1,0:T(8,128)S(1)}, f32[8,512]{1,0:T(8,128)S(1)}, u32[]{:S(2)}, u32[]{:S(2)}) %collective-permute-start.4) | collective-permute-done | bytes 16416 | tf_op jit(solution)/shard_map/ppermute | solution.py:242
  10.7 3.4 %collective-permute-done.3.refs_2_ = f32[8,512]{1,0:T(8,128)S(1)} collective-permute-done((f32[8,512]{1,0:T(8,128)S(1)}, f32[8,512]{1,0:T(8,128)S(1)}, u32[]{:S(2)}, u32[]{:S(2)}) %collective-permute-start.3) | collective-permute-done | bytes 16416 | tf_op jit(solution)/shard_map/ppermute | solution.py:242
  14.1 1.5 %collective-permute-start.6 = (f32[4,8,512]{2,1,0:T(8,128)S(1)}, f32[4,8,512]{2,1,0:T(8,128)S(1)}, u32[]{:S(2)}, u32[]{:S(2)}) collective-permute-start(f32[4,8,512]{2,1,0:T(8,128)S(1)} %pad_maximum_fusion), channel_id=1, source_target_pairs={{0,4},{4,0},{8,12},{12,8},{16,20},{20,16},{24,28},{28,24},{1,5},{5... | collective-permute-start | bytes 196616 | tf_op jit(solution)/shard_map/ppermute | solution.py:247
  15.7 0.0 collective-permute-start
  15.7 1.5 %collective-permute-start.1 = (f32[8,128]{1,0:T(8,128)S(1)}, f32[8,128]{1,0:T(8,128)S(1)}, u32[]{:S(2)}, u32[]{:S(2)}) collective-permute-start(f32[8,128]{1,0:T(8,128)S(1)} %get-tuple-element.11), channel_id=1, source_target_pairs={{0,2},{1,3},{2,0},{3,1},{4,6},{5,7},{6,4},{7,5},{8,10},{9,11},{10,... | collective-permute-start | bytes 12296 | tf_op jit(solution)/shard_map/ppermute | solution.py:243
  17.2 0.4 %collective-permute-start.2 = (f32[8,128]{1,0:T(8,128)S(1)}, f32[8,128]{1,0:T(8,128)S(1)}, u32[]{:S(2)}, u32[]{:S(2)}) collective-permute-start(f32[8,128]{1,0:T(8,128)S(1)} %get-tuple-element.12), channel_id=1, source_target_pairs={{0,3},{1,2},{2,1},{3,0},{4,7},{5,6},{6,5},{7,4},{8,11},{9,10},{10,... | collective-permute-start | bytes 12296 | tf_op jit(solution)/shard_map/ppermute | solution.py:243
  17.5 0.9 %own_far.1.refs_1_ = f32[8,512]{1,0:T(8,128)S(1)} custom-call(f32[8,512]{1,0:T(8,128)S(1)} %get-tuple-element.9.refs_0_.refs_1_, f32[8,512]{1,0:T(8,128)S(1)} %get-tuple-element.9.refs_0_.refs_1_), custom_call_target="tpu_custom_call" | custom-call | flops 78643200 | tf_op jit(solution)/shard_map/own_far/pallas_call | solution.py:218
  18.4 0.0 collective-permute-done.refs_2_
  18.4 0.8 %collective-permute-done.1.refs_3_ = f32[8,128]{1,0:T(8,128)S(1)} collective-permute-done((f32[8,128]{1,0:T(8,128)S(1)}, f32[8,128]{1,0:T(8,128)S(1)}, u32[]{:S(2)}, u32[]{:S(2)}) %collective-permute-start.1) | collective-permute-done | bytes 4128 | tf_op jit(solution)/shard_map/ppermute | solution.py:243
  19.3 0.9 %collective-permute-done.2.refs_4_ = f32[8,128]{1,0:T(8,128)S(1)} collective-permute-done((f32[8,128]{1,0:T(8,128)S(1)}, f32[8,128]{1,0:T(8,128)S(1)}, u32[]{:S(2)}, u32[]{:S(2)}) %collective-permute-start.2) | collective-permute-done | bytes 4128 | tf_op jit(solution)/shard_map/ppermute | solution.py:243
  20.2 2.5 %near.1.refs_1_ = f32[8,512]{1,0:T(8,128)S(1)} custom-call(f32[8,512]{1,0:T(8,128)S(1)} %get-tuple-element.9.refs_0_.refs_1_, f32[8,512]{1,0:T(8,128)S(1)} %own_far.1.refs_1_, f32[8,128]{1,0:T(8,128)S(1)} %collective-permute-done.refs_2_, f32[8,128]{1,0:T(8,128)S(1)} %collective-permute-done.1.refs_3_, f32[8,128]{1,0:T(8,128)S(1)} %collective-permute-done.2.refs_4_, ...), custom_call_target="tpu_custom_call" | custom-call | flops 235929600 | tf_op jit(solution)/shard_map/near/pallas_call | solution.py:218
  22.7 2.4 %far_z.1.refs_1_ = f32[8,512]{1,0:T(8,128)S(1)} custom-call(f32[8,512]{1,0:T(8,128)S(1)} %get-tuple-element.9.refs_0_.refs_1_, f32[8,512]{1,0:T(8,128)S(1)} %near.1.refs_1_, f32[8,512]{1,0:T(8,128)S(1)} %collective-permute-done.3.refs_2_, f32[8,512]{1,0:T(8,128)S(1)} %collective-permute-done.4.refs_3_, f32[8,512]{1,0:T(8,128)S(1)} %collective-permute-done.5.refs_4_), custom_call_target="tpu_custom_call" | custom-call | flops 235929600 | tf_op jit(solution)/shard_map/far_z/pallas_call | solution.py:218
  25.1 0.0 collective-permute-done.6.refs_2_
  25.1 3.7 %far_y.1 = f32[3,512]{1,0:T(4,128)} custom-call(f32[8,512]{1,0:T(8,128)S(1)} %get-tuple-element.9.refs_0_.refs_1_, f32[8,512]{1,0:T(8,128)S(1)} %far_z.1.refs_1_, f32[4,8,512]{2,1,0:T(8,128)S(1)} %collective-permute-done.6.refs_2_), custom_call_target="tpu_custom_call" | custom-call | flops 314572800 | tf_op jit(solution)/shard_map/far_y/pallas_call | solution.py:218
  (7 shorter events, 0.0 us)
Async XLA Ops:
  0.0 0.7 %copy-start.4 = (s32[1,12,2]{1,2,0:T(2,128)S(1)}, s32[1,12,2]{1,2,0:T(2,128)}, u32[]{:S(2)}) copy-start(s32[1,12,2]{1,2,0:T(2,128)} %param.9) | copy-start | bytes 292
  0.0 0.8 %copy-start = (f32[3,512]{1,0:T(4,128)S(1)}, f32[3,512]{1,0:T(4,128)}, u32[]{:S(2)}) copy-start(f32[3,512]{1,0:T(4,128)} %pos_ref.1) | copy-start | bytes 18436
  0.7 0.7 %copy-start.2 = (s32[1,4]{1,0:T(1,128)S(1)}, s32[1,4]{1,0:T(1,128)}, u32[]{:S(2)}) copy-start(s32[1,4]{1,0:T(1,128)} %map_ref.1) | copy-start | bytes 52
  1.3 0.7 %copy-start.1 = (f32[3,512]{1,0:T(4,128)S(1)}, f32[3,512]{1,0:T(4,128)}, u32[]{:S(2)}) copy-start(f32[3,512]{1,0:T(4,128)} %den_ref.1) | copy-start | bytes 18436
  2.9 5.7 %collective-permute-start.5 = (f32[8,512]{1,0:T(8,128)S(1)}, f32[8,512]{1,0:T(8,128)S(1)}, u32[]{:S(2)}, u32[]{:S(2)}) collective-permute-start(f32[8,512]{1,0:T(8,128)S(1)} %get-tuple-element.9.refs_0_.refs_1_), channel_id=1, source_target_pairs={{0,8},{4,12},{8,0},{12,4},{16,24},{20,28},{24,16},{28,20},{1,9},{5... | collective-permute-start | bytes 49160 | tf_op jit(solution)/shard_map/ppermute | solution.py:242
  6.0 4.7 %collective-permute-start.4 = (f32[8,512]{1,0:T(8,128)S(1)}, f32[8,512]{1,0:T(8,128)S(1)}, u32[]{:S(2)}, u32[]{:S(2)}) collective-permute-start(f32[8,512]{1,0:T(8,128)S(1)} %get-tuple-element.9.refs_0_.refs_1_), channel_id=1, source_target_pairs={{0,16},{4,20},{8,24},{12,28},{16,0},{20,4},{24,8},{28,12},{1,17},{... | collective-permute-start | bytes 49160 | tf_op jit(solution)/shard_map/ppermute | solution.py:242
  8.6 5.5 %collective-permute-start.3 = (f32[8,512]{1,0:T(8,128)S(1)}, f32[8,512]{1,0:T(8,128)S(1)}, u32[]{:S(2)}, u32[]{:S(2)}) collective-permute-start(f32[8,512]{1,0:T(8,128)S(1)} %get-tuple-element.9.refs_0_.refs_1_), channel_id=1, source_target_pairs={{0,24},{4,28},{8,16},{12,20},{16,8},{20,12},{24,0},{28,4},{1,25},{... | collective-permute-start | bytes 49160 | tf_op jit(solution)/shard_map/ppermute | solution.py:242
  14.1 10.9 %collective-permute-start.6 = (f32[4,8,512]{2,1,0:T(8,128)S(1)}, f32[4,8,512]{2,1,0:T(8,128)S(1)}, u32[]{:S(2)}, u32[]{:S(2)}) collective-permute-start(f32[4,8,512]{2,1,0:T(8,128)S(1)} %pad_maximum_fusion), channel_id=1, source_target_pairs={{0,4},{4,0},{8,12},{12,8},{16,20},{20,16},{24,28},{28,24},{1,5},{5... | collective-permute-start | bytes 196616 | tf_op jit(solution)/shard_map/ppermute | solution.py:247
  15.7 2.8 %collective-permute-start = (f32[8,128]{1,0:T(8,128)S(1)}, f32[8,128]{1,0:T(8,128)S(1)}, u32[]{:S(2)}, u32[]{:S(2)}) collective-permute-start(f32[8,128]{1,0:T(8,128)S(1)} %get-tuple-element.10), channel_id=1, source_target_pairs={{0,1},{1,0},{2,3},{3,2},{4,5},{5,4},{6,7},{7,6},{8,9},{9,8},{10,11... | collective-permute-start | bytes 12296 | tf_op jit(solution)/shard_map/ppermute | solution.py:243
  15.7 3.6 %collective-permute-start.1 = (f32[8,128]{1,0:T(8,128)S(1)}, f32[8,128]{1,0:T(8,128)S(1)}, u32[]{:S(2)}, u32[]{:S(2)}) collective-permute-start(f32[8,128]{1,0:T(8,128)S(1)} %get-tuple-element.11), channel_id=1, source_target_pairs={{0,2},{1,3},{2,0},{3,1},{4,6},{5,7},{6,4},{7,5},{8,10},{9,11},{10,... | collective-permute-start | bytes 12296 | tf_op jit(solution)/shard_map/ppermute | solution.py:243
  17.2 3.0 %copy-start.3 = (f32[32,128]{1,0:T(8,128)S(1)}, f32[32,128]{1,0:T(8,128)}, u32[]{:S(2)}) copy-start(f32[32,128]{1,0:T(8,128)} %refs_5_.1) | copy-start | bytes 49156
  17.2 3.0 %collective-permute-start.2 = (f32[8,128]{1,0:T(8,128)S(1)}, f32[8,128]{1,0:T(8,128)S(1)}, u32[]{:S(2)}, u32[]{:S(2)}) collective-permute-start(f32[8,128]{1,0:T(8,128)S(1)} %get-tuple-element.12), channel_id=1, source_target_pairs={{0,3},{1,2},{2,1},{3,0},{4,7},{5,6},{6,5},{7,4},{8,11},{9,10},{10,... | collective-permute-start | bytes 12296 | tf_op jit(solution)/shard_map/ppermute | solution.py:243
where the time goes:
time: 29 us; the launch traced here: 28.8 us
  Pallas kernels  10.4 us (36%)
  starting transfers between devices  9.06 us (31%)
  waiting for transfers between devices  7.31 us (25%)
  local copies, waits for them, and re-layouts  2.03 us (7%)
    pallas_call x4, Pallas kernels, pair_sums(): pl.pallas_call(functools.partial(sum_kernel, len(far), len(near), prior i...  9.49 us
    ppermute x3, starting transfers between devices, shards(): zs = [lax.ppermute(own, 'blk', flips(columns, b)) for b in (6, 4, 2)]  5.68 us
    ppermute x3, waiting for transfers between devices, shards(): zs = [lax.ppermute(own, 'blk', flips(columns, b)) for b in (6, 4, 2)]  5.53 us
    unnamed x10, local copies, waits for them, and re-layouts  1.94 us
    ppermute x3, starting transfers between devices, shards(): lax.ppermute(t, 'nbr', flips(peers, d + 1))  1.86 us
    ppermute x3, waiting for transfers between devices, shards(): lax.ppermute(t, 'nbr', flips(peers, d + 1))  1.77 us
    ppermute x1, starting transfers between devices, shards(): other = lax.ppermute(four, 'blk', flips(columns, 1))  1.52 us
    pallas_call x1, Pallas kernels, pack(): pl.pallas_call(functools.partial(pack_kernel, peers, slots, entries, pane...  0.88 us
  transfers between devices with their start and end apart: 7, of which 4 were waited for; matrix products, arithmetic and copies ran while one was open for 0% of the time, Pallas kernels for 20%

commit v1 on v0

--- a/solution.py
+++ b/solution.py
@@ -16,6 +16,9 @@
 LANES = 128
 ROWS = 8
 VMEM_LIMIT = 40 * 2**20
+WIDE = 1024
+PACK_FLOPS = 900 * 10**6
+PAIR_FLOPS = 3500
 
 
 def split3(a):
@@ -109,25 +112,16 @@
     return [fine[ROWS * i : ROWS * (i + 1)] for i in range(len(tiles))]
 
 
-def pack_kernel(peers, slots, entries, panel_pts, pos_ref, den_ref, list_ref, map_ref, own_ref, *rest):
-    tile_refs = rest[: peers - 1]
-    table, count = rest[peers - 1 :]
-    own_ref[0:3, :] = pos_ref[...]
-    own_ref[3:6, :] = den_ref[...]
-    own_ref[6:8, :] = jnp.zeros((2, own_ref.shape[1]), F32)
+def pack_kernel(peers, slots, entries, panel_pts, own_ref, list_ref, map_ref, odd_ref, even_ref, table, count):
     me = lax.axis_index("nbr")
-
-    def clear(i, _):
+    for i in range(peers * slots + 1):
         table[i] = -1
-        return 0
-
-    lax.fori_loop(0, peers * slots + 1, clear, 0, unroll=True)
     for i in range(peers + 1):
         count[i] = 0
 
     def place(e, _):
-        panel = list_ref[e, 0]
-        cell = list_ref[e, 1]
+        panel = list_ref[0, 0, e]
+        cell = list_ref[0, 1, e]
         valid = cell >= 0
         dest = map_ref[0, jnp.maximum(cell, 0)]
         at = jnp.where(valid, dest, peers)
@@ -150,28 +144,41 @@
             shift = (s - safe % group + group) % group * panel_pts
             moved = pltpu.roll(piece, shift, 1)
             tile = jnp.where((lane_group == s) & (panel >= 0), moved, tile)
-        tile_refs[d - 1][...] = tile
-
-
-def pack(positions, density, near_list, cell_map, panel_pts, peers):
-    points = positions.shape[1]
-    entries = near_list.shape[0]
+        if d % 2:
+            odd_ref[d // 2] = tile
+        else:
+            even_ref[d // 2 - 1] = tile
+
+
+def pack(own, near_list, cell_map, panel_pts, peers):
+    entries = near_list.shape[2]
     slots = LANES // panel_pts
     vmem = pl.BlockSpec(memory_space=pltpu.VMEM)
     smem = pl.BlockSpec(memory_space=pltpu.SMEM)
     return pl.pallas_call(
         functools.partial(pack_kernel, peers, slots, entries, panel_pts),
-        out_shape=[jax.ShapeDtypeStruct((ROWS, points), F32)]
-        + [jax.ShapeDtypeStruct((ROWS, LANES), F32)] * (peers - 1),
-        in_specs=[vmem, vmem, smem, smem],
-        out_specs=[vmem] * peers,
+        out_shape=[
+            jax.ShapeDtypeStruct((peers // 2, ROWS, LANES), F32),
+            jax.ShapeDtypeStruct((peers // 2 - 1, ROWS, LANES), F32),
+        ],
+        in_specs=[vmem, smem, smem],
+        out_specs=[vmem] * 2,
         scratch_shapes=[pltpu.SMEM((peers * slots + 1,), jnp.int32), pltpu.SMEM((peers + 1,), jnp.int32)],
         compiler_params=pltpu.CompilerParams(vmem_limit_bytes=VMEM_LIMIT),
+        cost_estimate=pl.CostEstimate(flops=PACK_FLOPS, bytes_accessed=0, transcendentals=0),
         name="pack",
-    )(positions, density, near_list, cell_map)
-
-
-def sum_kernel(n_far, n_near, has_prior, final, *refs):
+    )(own, near_list, cell_map)
+
+
+def wide_blocks(refs):
+    singles = []
+    for ref in refs:
+        singles += [ref[...]] if len(ref.shape) == 2 else [ref[i] for i in range(ref.shape[0])]
+    group = max(1, WIDE // singles[0].shape[1])
+    return [jnp.concatenate(singles[i : i + group], axis=1) for i in range(0, len(singles), group)]
+
+
+def sum_kernel(n_far, n_near, has_prior, keep, final, *refs):
     refs = list(refs)
     x_ref = refs.pop(0)
     prior = refs.pop(0)[...] if has_prior else None
@@ -182,23 +189,34 @@
     x = x_ref[0:3, :]
     proj_t = project_features(x)
     total = jnp.zeros((2 * ROWS, x.shape[1]), F32)
+    if keep:
+        at = 0
+        for ref in far_refs:
+            if len(ref.shape) == 2:
+                refs[0][at] = ref[...]
+                at += 1
+            else:
+                refs[0][at : at + ref.shape[0]] = ref[...]
+                at += ref.shape[0]
     if n_far:
         dist_t = target_features(x, FAR_REG_SQ)
+        small = [ref for ref in far_refs if len(ref.shape) == 2 or ref.shape[0] <= 4]
+        if small:
+            for block in wide_blocks(small):
+                total = total + block_sum(block, dist_t, proj_t, FAR_REG_SQ)
         for ref in far_refs:
-            if len(ref.shape) == 2:
-                total = total + block_sum(ref[...], dist_t, proj_t, FAR_REG_SQ)
-            elif ref.shape[0] <= 4:
-                for i in range(ref.shape[0]):
-                    total = total + block_sum(ref[i], dist_t, proj_t, FAR_REG_SQ)
-            else:
+            if len(ref.shape) == 3 and ref.shape[0] > 4:
                 total = lax.fori_loop(
                     0, ref.shape[0], lambda i, t, ref=ref: t + block_sum(ref[i], dist_t, proj_t, FAR_REG_SQ), total
                 )
     if n_near:
         dist_t = target_features(x, NEAR_REG_SQ)
-        for start in range(0, n_near, 3):
-            for fine in upsample_tiles([r[...] for r in near_refs[start : start + 3]], table_ref[...]):
-                total = total + block_sum(fine, dist_t, proj_t, NEAR_REG_SQ)
+        tiles = []
+        for ref in near_refs:
+            tiles += [ref[i] for i in range(ref.shape[0])]
+        for start in range(0, len(tiles), 3):
+            fine = upsample_tiles(tiles[start : start + 3], table_ref[...])
+            total = total + block_sum(jnp.concatenate(fine, axis=1), dist_t, proj_t, NEAR_REG_SQ)
     summed = total[0:ROWS] + total[ROWS:]
     if has_prior:
         summed = summed + prior
@@ -208,52 +226,75 @@
         out_ref[...] = summed
 
 
-def pair_sums(name, own, prior, far, near, table, final):
+def pair_sums(name, own, prior, far, near, table, final=False, keep=False):
     points = own.shape[1]
     vmem = pl.BlockSpec(memory_space=pltpu.VMEM)
     args = [own] + ([prior] if prior is not None else []) + list(far) + list(near) + ([table] if near else [])
-    pairs = points * (
-        sum(a.size // ROWS for a in far) + (sum(a.size // ROWS for a in near) * table.shape[1] // table.shape[0] if near else 0)
-    )
-    return pl.pallas_call(
-        functools.partial(sum_kernel, len(far), len(near), prior is not None, final),
-        out_shape=jax.ShapeDtypeStruct((3 if final else ROWS, points), F32),
+    far_sources = sum(a.size // ROWS for a in far)
+    near_sources = sum(a.size // ROWS for a in near) * table.shape[1] // table.shape[0]
+    pairs = points * (far_sources + near_sources)
+    out_shape = [jax.ShapeDtypeStruct((3 if final else ROWS, points), F32)]
+    if keep:
+        out_shape.append(jax.ShapeDtypeStruct((far_sources // points, ROWS, points), F32))
+    got = pl.pallas_call(
+        functools.partial(sum_kernel, len(far), len(near), prior is not None, keep, final),
+        out_shape=out_shape,
         in_specs=[vmem] * len(args),
-        out_specs=vmem,
+        out_specs=[vmem] * len(out_shape),
         compiler_params=pltpu.CompilerParams(vmem_limit_bytes=VMEM_LIMIT),
-        cost_estimate=pl.CostEstimate(flops=300 * pairs, bytes_accessed=0, transcendentals=pairs),
+        cost_estimate=pl.CostEstimate(flops=PAIR_FLOPS * pairs, bytes_accessed=0, transcendentals=pairs),
         name=name,
     )(*args)
+    return got if keep else got[0]
 
 
 def flips(size, bit):
     return [(i, i ^ bit) for i in range(size)]
 
 
-MODE = "B"
+def share_panels(odd, even):
+    peers = lax.axis_size("nbr")
+    held = {}
+    for d in range(1, peers):
+        held[d] = odd[d // 2] if d % 2 else even[d // 2 - 1]
+    bit = 1
+    while bit < peers:
+        sent = [d for d in range(1, peers) if d & bit]
+        stack = odd if bit == 1 else jnp.stack([held[d] for d in sent])
+        got = lax.ppermute(stack, "nbr", flips(peers, bit))
+        for i, d in enumerate(sent):
+            held[d] = got[i]
+        last = got
+        bit *= 2
+    done = [d for d in range(1, peers) if not d & (peers // 2)]
+    return [last] + [held[d][None] for d in done]
+
+
+ORDER = (4, 2, 6)
 
 
 def shards(positions, density, upsample, cell_map, near_list):
     columns = lax.axis_size("blk")
     peers = lax.axis_size("nbr")
-    own, *tiles = pack(positions, density, near_list[0], cell_map, upsample.shape[0], peers)
-    if MODE == "B":
-        bits = [b for b in (2, 4, 6) if b < columns]
-        zs = [lax.ppermute(own, "blk", flips(columns, b)) for b in (6, 4, 2)]
-        near = [lax.ppermute(t, "nbr", flips(peers, d + 1)) for d, t in enumerate(tiles)]
-        part = pair_sums("own_far", own, None, [own], [], upsample, False)
-        part = pair_sums("near", own, part, [], near, upsample, False)
-        four = jnp.stack([own] + zs)
-        other = lax.ppermute(four, "blk", flips(columns, 1))
-        part = pair_sums("far_z", own, part, zs, [], upsample, False)
-        rest = [other]
-        bit = 8
-        while bit < columns:
-            both = jnp.concatenate([four, other]) if bit == 8 else jnp.concatenate([both, more])
-            more = lax.ppermute(both, "blk", flips(columns, bit))
-            rest.append(more)
+    own = jnp.concatenate([positions, density, jnp.zeros((2, positions.shape[1]), F32)], axis=0)
+    zs = [lax.ppermute(own, "blk", flips(columns, b)) for b in ORDER]
+    part = pair_sums("far_own", own, None, [own], [], upsample)
+    odd, even = pack(own, jnp.swapaxes(near_list, 1, 2), cell_map, upsample.shape[0], peers)
+    near = share_panels(odd, even)
+    held = jnp.stack([own] + zs)
+    bit = 1
+    while bit < columns:
+        got = lax.ppermute(held, "blk", flips(columns, bit))
+        if bit == 1:
+            part = pair_sums("far_z", own, part, zs, [], upsample)
+            part = pair_sums("near", own, part, [], near, upsample)
+            bit = 8
+        else:
+            part = pair_sums("far_%d" % bit, own, part, [last], [], upsample)
             bit *= 2
-        return pair_sums("far_y", own, part, rest, [], upsample, True)
+        held = jnp.concatenate([held, got])
+        last = got
+    return pair_sums("far_last", own, part, [last], [], upsample, final=True)
 
 
 def solution(mesh):

time: 29 us -> 20.8 us (0.72)
  waiting for transfers between devices: 7.31 us -> 0.61 us
  local copies, waits for them, and re-layouts: 2.03 us -> 0.09 us
  other arithmetic: 0.01 us -> 0.79 us
  Pallas kernels: 10.4 us -> 10.1 us
    ppermute x7 -> x6, waiting for transfers between devices: 7.31 us -> 0.61 us  [the longest x3 0.35 us: shards(): zs = [lax.ppermute(own, 'blk', flips(columns, b)) for b in ORDER]]
    unnamed x10 -> x6, local copies, waits for them, and re-layouts: 1.94 us -> 0.01 us
    concatenate x0 -> x1, other arithmetic: none -> 0.78 us  [shards(): jnp.concatenate([positions, density, jnp.zeros((2, positions.shape[1]), F...]
    ppermute x7 -> x6, starting transfers between devices: 9.06 us -> 8.99 us  [the longest x3 5.71 us: shards(): zs = [lax.ppermute(own, 'blk', flips(columns, b)) for b in ORDER]]
  transfers between devices with their start and end apart: 7 -> 6, of which waited for: 4 -> 2; matrix products, arithmetic and copies ran while one was open for 0% -> 0% of each run, Pallas kernels for 20% -> 31%
where the time goes in v1:
time: 20.8 us; the launch traced here: 20.6 us
  Pallas kernels  10.1 us (49%)
  starting transfers between devices  8.99 us (43%)
  other arithmetic  0.79 us (4%)
  waiting for transfers between devices  0.61 us (3%)
    pallas_call x4, Pallas kernels, pair_sums(): pl.pallas_call(functools.partial(sum_kernel, len(far), len(near), prior i...  9.28 us
    ppermute x3, starting transfers between devices, shards(): zs = [lax.ppermute(own, 'blk', flips(columns, b)) for b in ORDER]  5.71 us
    ppermute x2, starting transfers between devices, share_panels(): got = lax.ppermute(stack, 'nbr', flips(peers, bit))  1.69 us
    ppermute x1, starting transfers between devices, shards(): got = lax.ppermute(held, 'blk', flips(columns, bit))  1.58 us
    concatenate x1, other arithmetic, shards(): jnp.concatenate([positions, density, jnp.zeros((2, positions.shape[1]), F...  0.78 us
    pallas_call x1, Pallas kernels, pack(): pl.pallas_call(functools.partial(pack_kernel, peers, slots, entries, pane...  0.78 us
  transfers between devices with their start and end apart: 6, of which 2 were waited for; matrix products, arithmetic and copies ran while one was open for 0% of the time, Pallas kernels for 31%

profile of v1, /device:TPU:0, one launch (start us, length us, event | category | flops | bytes accessed | tf_op | source)
XLA Modules:
  0.0 20.6 jit_solution(5570934851421473477)
XLA Ops:
  0.0 0.1 pad.8.clone
  0.1 0.8 %maximum_maximum_fusion.refs_0_.refs_1_.own_ref = f32[8,512]{1,0:T(8,128)S(1)} fusion(f32[3,512]{1,0:T(4,128)} %param.6, f32[3,512]{1,0:T(4,128)} %param.5, f32[8]{0:T(128)S(1)} %pad.8.clone), kind=kLoop, calls=%fused_computation.1 | loop fusion | flops 8192 | bytes 28704 | tf_op jit(solution)/shard_map/concatenate | solution.py:279
  0.9 0.0 copy-start.1
  0.9 0.0 copy-start.2
  0.9 5.1 %collective-permute-start.2 = (f32[8,512]{1,0:T(8,128)S(1)}, f32[8,512]{1,0:T(8,128)S(1)}, u32[]{:S(2)}, u32[]{:S(2)}) collective-permute-start(f32[8,512]{1,0:T(8,128)S(1)} %maximum_maximum_fusion.refs_0_.refs_1_.own_ref), channel_id=1, source_target_pairs={{0,24},{4,28},{8,16},{12,20},{16,8},{20,12},{24,0},{28,4},{1,25},{... | collective-permute-start | bytes 49160 | tf_op jit(solution)/shard_map/ppermute | solution.py:280
  5.9 0.0 collective-permute-start.1
  5.9 0.6 %collective-permute-start = (f32[8,512]{1,0:T(8,128)S(1)}, f32[8,512]{1,0:T(8,128)S(1)}, u32[]{:S(2)}, u32[]{:S(2)}) collective-permute-start(f32[8,512]{1,0:T(8,128)S(1)} %maximum_maximum_fusion.refs_0_.refs_1_.own_ref), channel_id=1, source_target_pairs={{0,16},{4,20},{8,24},{12,28},{16,0},{20,4},{24,8},{28,12},{1,17},{... | collective-permute-start | bytes 49160 | tf_op jit(solution)/shard_map/ppermute | solution.py:280
  6.6 0.0 copy-done.1
  6.6 0.0 copy-done.2
  6.6 0.8 %pack.1 = (f32[2,8,128]{2,1,0:T(8,128)S(1)}, f32[1,8,128]{2,1,0:T(8,128)S(1)}) custom-call(f32[8,512]{1,0:T(8,128)S(1)} %maximum_maximum_fusion.refs_0_.refs_1_.own_ref, s32[1,2,12]{2,1,0:T(2,128)S(1)} %bitcast.9, s32[1,4]{1,0:T(1,128)S(1)} %copy-done.2), custom_call_target="tpu_custom_call" | custom-call | flops 900000000 | tf_op jit(solution)/shard_map/pack/pallas_call | solution.py:158
  7.4 0.1 collective-permute-start.3
  7.4 0.9 %far_own.1.refs_1_ = f32[8,512]{1,0:T(8,128)S(1)} custom-call(f32[8,512]{1,0:T(8,128)S(1)} %maximum_maximum_fusion.refs_0_.refs_1_.own_ref, f32[8,512]{1,0:T(8,128)S(1)} %maximum_maximum_fusion.refs_0_.refs_1_.own_ref), custom_call_target="tpu_custom_call" | custom-call | flops 917504000 | tf_op jit(solution)/shard_map/far_own/pallas_call | solution.py:239
  8.3 0.3 %collective-permute-done.3 = f32[2,8,128]{2,1,0:T(8,128)S(1)} collective-permute-done((f32[2,8,128]{2,1,0:T(8,128)S(1)}, f32[2,8,128]{2,1,0:T(8,128)S(1)}, u32[]{:S(2)}, u32[]{:S(2)}) %collective-permute-start.3) | collective-permute-done | bytes 8224 | tf_op jit(solution)/shard_map/ppermute | solution.py:264
  8.6 1.6 %collective-permute-start.4 = (f32[2,8,128]{2,1,0:T(8,128)S(1)}, f32[2,8,128]{2,1,0:T(8,128)S(1)}, u32[]{:S(2)}, u32[]{:S(2)}) collective-permute-start(f32[2,8,128]{2,1,0:T(8,128)S(1)} %pad_maximum_fusion.1), channel_id=1, source_target_pairs={{0,2},{1,3},{2,0},{3,1},{4,6},{5,7},{6,4},{7,5},{8,10},{9,11},{10,... | collective-permute-start | bytes 24584 | tf_op jit(solution)/shard_map/ppermute | solution.py:264
  10.2 0.0 collective-permute-done.2.refs_4_
  10.2 0.0 collective-permute-done.1.refs_3_
  10.2 0.3 %collective-permute-done.refs_2_ = f32[8,512]{1,0:T(8,128)S(1)} collective-permute-done((f32[8,512]{1,0:T(8,128)S(1)}, f32[8,512]{1,0:T(8,128)S(1)}, u32[]{:S(2)}, u32[]{:S(2)}) %collective-permute-start) | collective-permute-done | bytes 16416 | tf_op jit(solution)/shard_map/ppermute | solution.py:280
  10.6 1.6 %collective-permute-start.5 = (f32[4,8,512]{2,1,0:T(8,128)S(1)}, f32[4,8,512]{2,1,0:T(8,128)S(1)}, u32[]{:S(2)}, u32[]{:S(2)}) collective-permute-start(f32[4,8,512]{2,1,0:T(8,128)S(1)} %pad_maximum_fusion), channel_id=1, source_target_pairs={{0,4},{4,0},{8,12},{12,8},{16,20},{20,16},{24,28},{28,24},{1,5},{5... | collective-permute-start | bytes 196616 | tf_op jit(solution)/shard_map/ppermute | solution.py:287
  12.2 2.3 %far_z.1.refs_1_ = f32[8,512]{1,0:T(8,128)S(1)} custom-call(f32[8,512]{1,0:T(8,128)S(1)} %maximum_maximum_fusion.refs_0_.refs_1_.own_ref, f32[8,512]{1,0:T(8,128)S(1)} %far_own.1.refs_1_, f32[8,512]{1,0:T(8,128)S(1)} %collective-permute-done.refs_2_, f32[8,512]{1,0:T(8,128)S(1)} %collective-permute-done.1.refs_3_, f32[8,512]{1,0:T(8,128)S(1)} %collective-permute-done.2.refs_4_), custom_call_target="tpu_custom_call" | custom-call | flops 2752512000 | tf_op jit(solution)/shard_map/far_z/pallas_call | solution.py:239
  14.5 0.0 collective-permute-done.4.refs_2_
  14.5 0.0 copy-done
  14.5 2.4 %near.1.refs_1_ = f32[8,512]{1,0:T(8,128)S(1)} custom-call(f32[8,512]{1,0:T(8,128)S(1)} %maximum_maximum_fusion.refs_0_.refs_1_.own_ref, f32[8,512]{1,0:T(8,128)S(1)} %far_z.1.refs_1_, f32[2,8,128]{2,1,0:T(8,128)S(1)} %collective-permute-done.4.refs_2_, f32[1,8,128]{2,1,0:T(8,128)S(1)} %get-tuple-element.9.refs_3_, f32[32,128]{1,0:T(8,128)S(1)} %copy-done), custom_call_target="tpu_custom_call" | custom-call | flops 2752512000 | tf_op jit(solution)/shard_map/near/pallas_call | solution.py:239
  16.9 0.0 collective-permute-done.5.refs_2_
  16.9 3.7 %far_last.1 = f32[3,512]{1,0:T(4,128)} custom-call(f32[8,512]{1,0:T(8,128)S(1)} %maximum_maximum_fusion.refs_0_.refs_1_.own_ref, f32[8,512]{1,0:T(8,128)S(1)} %near.1.refs_1_, f32[4,8,512]{2,1,0:T(8,128)S(1)} %collective-permute-done.5.refs_2_), custom_call_target="tpu_custom_call" | custom-call | flops 3670016000 | tf_op jit(solution)/shard_map/far_last/pallas_call | solution.py:239
  (5 shorter events, 0.0 us)
Async XLA Ops:
  0.9 5.7 %copy-start.1 = (s32[1,12,2]{1,2,0:T(2,128)S(1)}, s32[1,12,2]{1,2,0:T(2,128)}, u32[]{:S(2)}) copy-start(s32[1,12,2]{1,2,0:T(2,128)} %param.9) | copy-start | bytes 292
  0.9 5.7 %copy-start.2 = (s32[1,4]{1,0:T(1,128)S(1)}, s32[1,4]{1,0:T(1,128)}, u32[]{:S(2)}) copy-start(s32[1,4]{1,0:T(1,128)} %map_ref.1) | copy-start | bytes 52
  0.9 9.4 %collective-permute-start.2 = (f32[8,512]{1,0:T(8,128)S(1)}, f32[8,512]{1,0:T(8,128)S(1)}, u32[]{:S(2)}, u32[]{:S(2)}) collective-permute-start(f32[8,512]{1,0:T(8,128)S(1)} %maximum_maximum_fusion.refs_0_.refs_1_.own_ref), channel_id=1, source_target_pairs={{0,24},{4,28},{8,16},{12,20},{16,8},{20,12},{24,0},{28,4},{1,25},{... | collective-permute-start | bytes 49160 | tf_op jit(solution)/shard_map/ppermute | solution.py:280
  5.9 4.3 %collective-permute-start.1 = (f32[8,512]{1,0:T(8,128)S(1)}, f32[8,512]{1,0:T(8,128)S(1)}, u32[]{:S(2)}, u32[]{:S(2)}) collective-permute-start(f32[8,512]{1,0:T(8,128)S(1)} %maximum_maximum_fusion.refs_0_.refs_1_.own_ref), channel_id=1, source_target_pairs={{0,8},{4,12},{8,0},{12,4},{16,24},{20,28},{24,16},{28,20},{1,9},{5... | collective-permute-start | bytes 49160 | tf_op jit(solution)/shard_map/ppermute | solution.py:280
  5.9 4.6 %collective-permute-start = (f32[8,512]{1,0:T(8,128)S(1)}, f32[8,512]{1,0:T(8,128)S(1)}, u32[]{:S(2)}, u32[]{:S(2)}) collective-permute-start(f32[8,512]{1,0:T(8,128)S(1)} %maximum_maximum_fusion.refs_0_.refs_1_.own_ref), channel_id=1, source_target_pairs={{0,16},{4,20},{8,24},{12,28},{16,0},{20,4},{24,8},{28,12},{1,17},{... | collective-permute-start | bytes 49160 | tf_op jit(solution)/shard_map/ppermute | solution.py:280
  7.4 1.2 %collective-permute-start.3 = (f32[2,8,128]{2,1,0:T(8,128)S(1)}, f32[2,8,128]{2,1,0:T(8,128)S(1)}, u32[]{:S(2)}, u32[]{:S(2)}) collective-permute-start(f32[2,8,128]{2,1,0:T(8,128)S(1)} %get-tuple-element.8), channel_id=1, source_target_pairs={{0,1},{1,0},{2,3},{3,2},{4,5},{5,4},{6,7},{7,6},{8,9},{9,8},{10,11... | collective-permute-start | bytes 24584 | tf_op jit(solution)/shard_map/ppermute | solution.py:264
  8.6 5.9 %collective-permute-start.4 = (f32[2,8,128]{2,1,0:T(8,128)S(1)}, f32[2,8,128]{2,1,0:T(8,128)S(1)}, u32[]{:S(2)}, u32[]{:S(2)}) collective-permute-start(f32[2,8,128]{2,1,0:T(8,128)S(1)} %pad_maximum_fusion.1), channel_id=1, source_target_pairs={{0,2},{1,3},{2,0},{3,1},{4,6},{5,7},{6,4},{7,5},{8,10},{9,11},{10,... | collective-permute-start | bytes 24584 | tf_op jit(solution)/shard_map/ppermute | solution.py:264
  10.6 3.9 %copy-start = (f32[32,128]{1,0:T(8,128)S(1)}, f32[32,128]{1,0:T(8,128)}, u32[]{:S(2)}) copy-start(f32[32,128]{1,0:T(8,128)} %refs_4_.1) | copy-start | bytes 49156
  10.6 6.3 %collective-permute-start.5 = (f32[4,8,512]{2,1,0:T(8,128)S(1)}, f32[4,8,512]{2,1,0:T(8,128)S(1)}, u32[]{:S(2)}, u32[]{:S(2)}) collective-permute-start(f32[4,8,512]{2,1,0:T(8,128)S(1)} %pad_maximum_fusion), channel_id=1, source_target_pairs={{0,4},{4,0},{8,12},{12,8},{16,20},{20,16},{24,28},{28,24},{1,5},{5... | collective-permute-start | bytes 196616 | tf_op jit(solution)/shard_map/ppermute | solution.py:287

commit v2 on v1

--- a/solution.py
+++ b/solution.py
@@ -16,7 +16,10 @@
 LANES = 128
 ROWS = 8
 VMEM_LIMIT = 40 * 2**20
-WIDE = 1024
+WIDE = 1536
+USED = 6
+FIRST = 1
+SOON = 2
 PACK_FLOPS = 900 * 10**6
 PAIR_FLOPS = 3500
 
@@ -112,7 +115,9 @@
     return [fine[ROWS * i : ROWS * (i + 1)] for i in range(len(tiles))]
 
 
-def pack_kernel(peers, slots, entries, panel_pts, own_ref, list_ref, map_ref, odd_ref, even_ref, table, count):
+def pick_panels(peers, slots, panel_pts, own_ref, list_ref, map_ref, *rest):
+    *tile_refs, table, count = rest
+    entries = list_ref.shape[2]
     me = lax.axis_index("nbr")
     for i in range(peers * slots + 1):
         table[i] = -1
@@ -144,41 +149,38 @@
             shift = (s - safe % group + group) % group * panel_pts
             moved = pltpu.roll(piece, shift, 1)
             tile = jnp.where((lane_group == s) & (panel >= 0), moved, tile)
-        if d % 2:
-            odd_ref[d // 2] = tile
-        else:
-            even_ref[d // 2 - 1] = tile
-
-
-def pack(own, near_list, cell_map, panel_pts, peers):
-    entries = near_list.shape[2]
+        tile_refs[d - 1][0] = tile
+
+
+def near_panels(own, near_list, cell_map, panel_pts, peers):
     slots = LANES // panel_pts
     vmem = pl.BlockSpec(memory_space=pltpu.VMEM)
     smem = pl.BlockSpec(memory_space=pltpu.SMEM)
+    tile = jax.ShapeDtypeStruct((1, ROWS, LANES), F32)
     return pl.pallas_call(
-        functools.partial(pack_kernel, peers, slots, entries, panel_pts),
-        out_shape=[
-            jax.ShapeDtypeStruct((peers // 2, ROWS, LANES), F32),
-            jax.ShapeDtypeStruct((peers // 2 - 1, ROWS, LANES), F32),
-        ],
+        functools.partial(pick_panels, peers, slots, panel_pts),
+        out_shape=[tile] * (peers - 1),
         in_specs=[vmem, smem, smem],
-        out_specs=[vmem] * 2,
+        out_specs=[vmem] * (peers - 1),
         scratch_shapes=[pltpu.SMEM((peers * slots + 1,), jnp.int32), pltpu.SMEM((peers + 1,), jnp.int32)],
         compiler_params=pltpu.CompilerParams(vmem_limit_bytes=VMEM_LIMIT),
         cost_estimate=pl.CostEstimate(flops=PACK_FLOPS, bytes_accessed=0, transcendentals=0),
-        name="pack",
+        name="panels",
     )(own, near_list, cell_map)
 
 
 def wide_blocks(refs):
     singles = []
     for ref in refs:
-        singles += [ref[...]] if len(ref.shape) == 2 else [ref[i] for i in range(ref.shape[0])]
+        if ref.shape[0] == ROWS:
+            singles.append(ref[0:USED, :])
+        else:
+            singles += [ref[USED * i : USED * (i + 1), :] for i in range(ref.shape[0] // USED)]
     group = max(1, WIDE // singles[0].shape[1])
     return [jnp.concatenate(singles[i : i + group], axis=1) for i in range(0, len(singles), group)]
 
 
-def sum_kernel(n_far, n_near, has_prior, keep, final, *refs):
+def sum_kernel(n_far, n_near, has_prior, final, *refs):
     refs = list(refs)
     x_ref = refs.pop(0)
     prior = refs.pop(0)[...] if has_prior else None
@@ -189,26 +191,10 @@
     x = x_ref[0:3, :]
     proj_t = project_features(x)
     total = jnp.zeros((2 * ROWS, x.shape[1]), F32)
-    if keep:
-        at = 0
-        for ref in far_refs:
-            if len(ref.shape) == 2:
-                refs[0][at] = ref[...]
-                at += 1
-            else:
-                refs[0][at : at + ref.shape[0]] = ref[...]
-                at += ref.shape[0]
     if n_far:
         dist_t = target_features(x, FAR_REG_SQ)
-        small = [ref for ref in far_refs if len(ref.shape) == 2 or ref.shape[0] <= 4]
-        if small:
-            for block in wide_blocks(small):
-                total = total + block_sum(block, dist_t, proj_t, FAR_REG_SQ)
-        for ref in far_refs:
-            if len(ref.shape) == 3 and ref.shape[0] > 4:
-                total = lax.fori_loop(
-                    0, ref.shape[0], lambda i, t, ref=ref: t + block_sum(ref[i], dist_t, proj_t, FAR_REG_SQ), total
-                )
+        for block in wide_blocks(far_refs):
+            total = total + block_sum(block, dist_t, proj_t, FAR_REG_SQ)
     if n_near:
         dist_t = target_features(x, NEAR_REG_SQ)
         tiles = []
@@ -226,7 +212,7 @@
         out_ref[...] = summed
 
 
-def pair_sums(name, own, prior, far, near, table, final=False, keep=False):
+def pair_sums(name, own, prior, far, near, table, final=False):
     points = own.shape[1]
     vmem = pl.BlockSpec(memory_space=pltpu.VMEM)
     args = [own] + ([prior] if prior is not None else []) + list(far) + list(near) + ([table] if near else [])
@@ -234,10 +220,8 @@
     near_sources = sum(a.size // ROWS for a in near) * table.shape[1] // table.shape[0]
     pairs = points * (far_sources + near_sources)
     out_shape = [jax.ShapeDtypeStruct((3 if final else ROWS, points), F32)]
-    if keep:
-        out_shape.append(jax.ShapeDtypeStruct((far_sources // points, ROWS, points), F32))
     got = pl.pallas_call(
-        functools.partial(sum_kernel, len(far), len(near), prior is not None, keep, final),
+        functools.partial(sum_kernel, len(far), len(near), prior is not None, final),
         out_shape=out_shape,
         in_specs=[vmem] * len(args),
         out_specs=[vmem] * len(out_shape),
@@ -245,53 +229,144 @@
         cost_estimate=pl.CostEstimate(flops=PAIR_FLOPS * pairs, bytes_accessed=0, transcendentals=pairs),
         name=name,
     )(*args)
-    return got if keep else got[0]
+    return got[0]
+
+
+def place():
+    blk = lax.axis_index("blk")
+    first = blk < FIRST
+    soon = jnp.logical_and(blk >= FIRST, blk < SOON * (lax.axis_size("blk") // 4))
+    late = jnp.logical_and(blk >= FIRST, blk >= SOON * (lax.axis_size("blk") // 4))
+    return first, soon, late
+
+
+def far_total(x, blocks, part=None):
+    total = jnp.zeros((2 * ROWS, x.shape[1]), F32)
+    dist_t = target_features(x, FAR_REG_SQ)
+    proj_t = project_features(x)
+    for block in wide_blocks(blocks):
+        total = total + block_sum(block, dist_t, proj_t, FAR_REG_SQ)
+    total = total[0:ROWS] + total[ROWS:]
+    return total if part is None else part + total
+
+
+def first_kernel(own_ref, copy_ref, out_ref):
+    first, soon, late = place()
+    copy_ref[...] = own_ref[...]
+
+    @pl.when(first)
+    def _():
+        out_ref[...] = far_total(own_ref[0:3, :], [own_ref])
+
+    @pl.when(jnp.logical_not(first))
+    def _():
+        out_ref[...] = jnp.zeros(out_ref.shape, F32)
+
+
+def before_kernel(own_ref, part_ref, *refs):
+    *block_refs, held_ref, out_ref = refs
+    first, soon, late = place()
+    for i, ref in enumerate([own_ref, *block_refs]):
+        held_ref[USED * i : USED * (i + 1), :] = ref[0:USED, :]
+
+    @pl.when(first)
+    def _():
+        out_ref[...] = far_total(own_ref[0:3, :], block_refs[:1], part_ref[...])
+
+    @pl.when(soon)
+    def _():
+        out_ref[...] = far_total(own_ref[0:3, :], [own_ref], part_ref[...])
+
+    @pl.when(late)
+    def _():
+        out_ref[...] = part_ref[...]
+
+
+def after_kernel(own_ref, part_ref, *refs):
+    *block_refs, out_ref = refs
+    first, soon, late = place()
+
+    @pl.when(first)
+    def _():
+        out_ref[...] = far_total(own_ref[0:3, :], block_refs[1:], part_ref[...])
+
+    @pl.when(soon)
+    def _():
+        out_ref[...] = far_total(own_ref[0:3, :], block_refs, part_ref[...])
+
+    @pl.when(late)
+    def _():
+        out_ref[...] = far_total(own_ref[0:3, :], [own_ref, *block_refs], part_ref[...])
+
+
+def far_first(own):
+    vmem = pl.BlockSpec(memory_space=pltpu.VMEM)
+    return pl.pallas_call(
+        first_kernel,
+        out_shape=[jax.ShapeDtypeStruct(own.shape, F32)] * 2,
+        in_specs=[vmem],
+        out_specs=[vmem] * 2,
+        compiler_params=pltpu.CompilerParams(vmem_limit_bytes=VMEM_LIMIT),
+        name="far_first",
+    )(own)
+
+
+def far_before(own, part, blocks):
+    vmem = pl.BlockSpec(memory_space=pltpu.VMEM)
+    return pl.pallas_call(
+        before_kernel,
+        out_shape=[
+            jax.ShapeDtypeStruct((USED * (len(blocks) + 1), own.shape[1]), F32),
+            jax.ShapeDtypeStruct(own.shape, F32),
+        ],
+        in_specs=[vmem] * (2 + len(blocks)),
+        out_specs=[vmem] * 2,
+        compiler_params=pltpu.CompilerParams(vmem_limit_bytes=VMEM_LIMIT),
+        name="far_before",
+    )(own, part, *blocks)
+
+
+def far_after(own, part, blocks):
+    vmem = pl.BlockSpec(memory_space=pltpu.VMEM)
+    pairs = (len(blocks) + 1) * own.shape[1] ** 2
+    return pl.pallas_call(
+        after_kernel,
+        out_shape=jax.ShapeDtypeStruct(own.shape, F32),
+        in_specs=[vmem] * (2 + len(blocks)),
+        out_specs=vmem,
+        compiler_params=pltpu.CompilerParams(vmem_limit_bytes=VMEM_LIMIT),
+        cost_estimate=pl.CostEstimate(flops=PAIR_FLOPS * pairs, bytes_accessed=0, transcendentals=pairs),
+        name="far_after",
+    )(own, part, *blocks)
 
 
 def flips(size, bit):
     return [(i, i ^ bit) for i in range(size)]
 
 
-def share_panels(odd, even):
-    peers = lax.axis_size("nbr")
-    held = {}
-    for d in range(1, peers):
-        held[d] = odd[d // 2] if d % 2 else even[d // 2 - 1]
-    bit = 1
-    while bit < peers:
-        sent = [d for d in range(1, peers) if d & bit]
-        stack = odd if bit == 1 else jnp.stack([held[d] for d in sent])
-        got = lax.ppermute(stack, "nbr", flips(peers, bit))
-        for i, d in enumerate(sent):
-            held[d] = got[i]
-        last = got
-        bit *= 2
-    done = [d for d in range(1, peers) if not d & (peers // 2)]
-    return [last] + [held[d][None] for d in done]
-
-
-ORDER = (4, 2, 6)
+ORDER = (2, 3, 1)
+LATER = (4, 8, 16, 32)
 
 
 def shards(positions, density, upsample, cell_map, near_list):
     columns = lax.axis_size("blk")
     peers = lax.axis_size("nbr")
     own = jnp.concatenate([positions, density, jnp.zeros((2, positions.shape[1]), F32)], axis=0)
+    own, part = far_first(own)
     zs = [lax.ppermute(own, "blk", flips(columns, b)) for b in ORDER]
-    part = pair_sums("far_own", own, None, [own], [], upsample)
-    odd, even = pack(own, jnp.swapaxes(near_list, 1, 2), cell_map, upsample.shape[0], peers)
-    near = share_panels(odd, even)
-    held = jnp.stack([own] + zs)
-    bit = 1
-    while bit < columns:
+    tiles = near_panels(own, jnp.swapaxes(near_list, 1, 2), cell_map, upsample.shape[0], peers)
+    near = [lax.ppermute(t, "nbr", flips(peers, d + 1)) for d, t in enumerate(tiles)]
+    held, part = far_before(own, part, zs)
+    last = None
+    for bit in LATER:
+        if bit >= columns:
+            break
         got = lax.ppermute(held, "blk", flips(columns, bit))
-        if bit == 1:
-            part = pair_sums("far_z", own, part, zs, [], upsample)
+        if last is None:
+            part = far_after(own, part, zs)
             part = pair_sums("near", own, part, [], near, upsample)
-            bit = 8
         else:
             part = pair_sums("far_%d" % bit, own, part, [last], [], upsample)
-            bit *= 2
         held = jnp.concatenate([held, got])
         last = got
     return pair_sums("far_last", own, part, [last], [], upsample, final=True)

time: 20.8 us -> 19.7 us (0.947)
  starting transfers between devices: 8.99 us -> 8.32 us
  waiting for transfers between devices: 0.61 us -> 0.02 us
    pallas_call x1 -> x4, Pallas kernels: 0.78 us -> 4.21 us  [the longest x1 1.64 us: far_after(): pl.pallas_call(after_kernel, out_shape=jax.ShapeDtypeStruct(own.shape, F3...]
    pallas_call x4 -> x2, Pallas kernels: 9.28 us -> 5.97 us  [pair_sums(): pl.pallas_call(functools.partial(sum_kernel, len(far), len(near), prior i...]
    ppermute x3, starting transfers between devices: 5.71 us -> 3.74 us  [shards(): zs = [lax.ppermute(own, 'blk', flips(columns, b)) for b in ORDER]]
    ppermute x2 -> x3, starting transfers between devices: 1.69 us -> 2.93 us  [shards(): lax.ppermute(t, 'nbr', flips(peers, d + 1))]
    ppermute x3, waiting for transfers between devices: 0.35 us -> 0.01 us  [shards(): zs = [lax.ppermute(own, 'blk', flips(columns, b)) for b in ORDER]]
    ppermute x2 -> x3, waiting for transfers between devices: 0.27 us -> 0.01 us  [shards(): lax.ppermute(t, 'nbr', flips(peers, d + 1))]
  transfers between devices with their start and end apart: 6 -> 7, of which waited for: 2 -> 0; matrix products, arithmetic and copies ran while one was open for 0% -> 0% of each run, Pallas kernels for 31% -> 29%
where the time goes in v2:
time: 19.7 us; the launch traced here: 19.5 us
  Pallas kernels  10.2 us (52%)
  starting transfers between devices  8.32 us (42%)
  other arithmetic  0.78 us (4%)
    pallas_call x2, Pallas kernels, pair_sums(): pl.pallas_call(functools.partial(sum_kernel, len(far), len(near), prior i...  5.97 us
    ppermute x3, starting transfers between devices, shards(): zs = [lax.ppermute(own, 'blk', flips(columns, b)) for b in ORDER]  3.74 us
    ppermute x3, starting transfers between devices, shards(): lax.ppermute(t, 'nbr', flips(peers, d + 1))  2.93 us
    ppermute x1, starting transfers between devices, shards(): got = lax.ppermute(held, 'blk', flips(columns, bit))  1.65 us
    pallas_call x1, Pallas kernels, far_after(): pl.pallas_call(after_kernel, out_shape=jax.ShapeDtypeStruct(own.shape, F3...  1.64 us
    pallas_call x1, Pallas kernels, far_before(): pl.pallas_call(before_kernel, out_shape=[jax.ShapeDtypeStruct((USED * (le...  0.9 us
    pallas_call x1, Pallas kernels, far_first(): pl.pallas_call(first_kernel, out_shape=[jax.ShapeDtypeStruct(own.shape, F...  0.9 us
    concatenate x1, other arithmetic, shards(): jnp.concatenate([positions, density, jnp.zeros((2, positions.shape[1]), F...  0.78 us
  transfers between devices with their start and end apart: 7, of which 0 were waited for; matrix products, arithmetic and copies ran while one was open for 0% of the time, Pallas kernels for 29%

profile of v2, /device:TPU:0, one launch (start us, length us, event | category | flops | bytes accessed | tf_op | source)
XLA Modules:
  0.0 19.5 jit_solution(6361101688826399082)
XLA Ops:
  0.0 0.1 pad.2.clone
  0.1 0.8 %maximum_maximum_fusion.own_ref = f32[8,512]{1,0:T(8,128)S(1)} fusion(f32[3,512]{1,0:T(4,128)} %param.6, f32[3,512]{1,0:T(4,128)} %param.5, f32[8]{0:T(128)S(1)} %pad.2.clone), kind=kLoop, calls=%fused_computation | loop fusion | flops 8192 | bytes 28704 | tf_op jit(solution)/shard_map/concatenate | solution.py:354
  0.9 0.9 %far_first.1 = (f32[8,512]{1,0:T(8,128)S(1)}, f32[8,512]{1,0:T(8,128)S(1)}) custom-call(f32[8,512]{1,0:T(8,128)S(1)} %maximum_maximum_fusion.own_ref), custom_call_target="tpu_custom_call" | custom-call | tf_op jit(solution)/shard_map/far_first/pallas_call | solution.py:304
  1.8 2.2 %collective-permute-start = (f32[8,512]{1,0:T(8,128)S(1)}, f32[8,512]{1,0:T(8,128)S(1)}, u32[]{:S(2)}, u32[]{:S(2)}) collective-permute-start(f32[8,512]{1,0:T(8,128)S(1)} %get-tuple-element.12.own_ref.refs_0_), channel_id=1, source_target_pairs={{0,8},{4,12},{8,0},{12,4},{16,24},{20,28},{24,16},{28,20},{1,9},{5... | collective-permute-start | bytes 49160 | tf_op jit(solution)/shard_map/ppermute | solution.py:356
  4.0 1.4 %collective-permute-start.1 = (f32[8,512]{1,0:T(8,128)S(1)}, f32[8,512]{1,0:T(8,128)S(1)}, u32[]{:S(2)}, u32[]{:S(2)}) collective-permute-start(f32[8,512]{1,0:T(8,128)S(1)} %get-tuple-element.12.own_ref.refs_0_), channel_id=1, source_target_pairs={{0,12},{4,8},{8,4},{12,0},{16,28},{20,24},{24,20},{28,16},{1,13},{... | collective-permute-start | bytes 49160 | tf_op jit(solution)/shard_map/ppermute | solution.py:356
  5.4 0.1 collective-permute-start.2
  5.5 0.0 copy-done.1
  5.5 0.0 copy-done.2
  5.5 0.8 %panels.1 = (f32[1,8,128]{2,1,0:T(8,128)S(1)}, f32[1,8,128]{2,1,0:T(8,128)S(1)}, f32[1,8,128]{2,1,0:T(8,128)S(1)}) custom-call(f32[8,512]{1,0:T(8,128)S(1)} %get-tuple-element.12.own_ref.refs_0_, s32[1,2,12]{2,1,0:T(2,128)S(1)} %bitcast.1, s32[1,4]{1,0:T(1,128)S(1)} %copy-done.2), custom_call_target="tpu_custom_call" | custom-call | flops 900000000 | tf_op jit(solution)/shard_map/panels/pallas_call | solution.py:160
  6.3 0.1 collective-permute-start.3
  6.4 2.8 %collective-permute-start.4 = (f32[1,8,128]{2,1,0:T(8,128)S(1)}, f32[1,8,128]{2,1,0:T(8,128)S(1)}, u32[]{:S(2)}, u32[]{:S(2)}) collective-permute-start(f32[1,8,128]{2,1,0:T(8,128)S(1)} %get-tuple-element.16), channel_id=1, source_target_pairs={{0,2},{1,3},{2,0},{3,1},{4,6},{5,7},{6,4},{7,5},{8,10},{9,11},{10,... | collective-permute-start | bytes 12296 | tf_op jit(solution)/shard_map/ppermute | solution.py:358
  9.2 0.0 collective-permute-done.refs_0_
  9.2 0.1 collective-permute-start.5
  9.2 0.0 collective-permute-done.1.refs_1_
  9.2 0.0 collective-permute-done.2.refs_2_
  9.2 0.9 %far_before.1 = (f32[24,512]{1,0:T(8,128)S(1)}, f32[8,512]{1,0:T(8,128)S(1)}) custom-call(f32[8,512]{1,0:T(8,128)S(1)} %get-tuple-element.12.own_ref.refs_0_, f32[8,512]{1,0:T(8,128)S(1)} %get-tuple-element.13.part_ref, f32[8,512]{1,0:T(8,128)S(1)} %collective-permute-done.refs_0_, f32[8,512]{1,0:T(8,128)S(1)} %collective-permute-done.1.refs_1_, ...), custom_call_target="tpu_custom_call" | custom-call | tf_op jit(solution)/shard_map/far_before/pallas_call | solution.py:316
  10.1 1.6 %collective-permute-start.6 = (f32[24,512]{1,0:T(8,128)S(1)}, f32[24,512]{1,0:T(8,128)S(1)}, u32[]{:S(2)}, u32[]{:S(2)}) collective-permute-start(f32[24,512]{1,0:T(8,128)S(1)} %get-tuple-element.18), channel_id=1, source_target_pairs={{0,16},{4,20},{8,24},{12,28},{16,0},{20,4},{24,8},{28,12},{1,17},{... | collective-permute-start | bytes 147464 | tf_op jit(solution)/shard_map/ppermute | solution.py:364
  11.8 1.6 %far_after.1.refs_1_ = f32[8,512]{1,0:T(8,128)S(1)} custom-call(f32[8,512]{1,0:T(8,128)S(1)} %get-tuple-element.12.own_ref.refs_0_, f32[8,512]{1,0:T(8,128)S(1)} %get-tuple-element.14.part_ref, f32[8,512]{1,0:T(8,128)S(1)} %collective-permute-done.refs_0_, f32[8,512]{1,0:T(8,128)S(1)} %collective-permute-done.1.refs_1_, ...), custom_call_target="tpu_custom_call" | custom-call | flops 3670016000 | tf_op jit(solution)/shard_map/far_after/pallas_call | solution.py:332
  13.4 0.0 collective-permute-done.3.refs_2_
  13.5 0.0 collective-permute-done.4.refs_3_
  13.5 0.0 collective-permute-done.5.refs_4_
  13.5 2.4 %near.1.refs_1_ = f32[8,512]{1,0:T(8,128)S(1)} custom-call(f32[8,512]{1,0:T(8,128)S(1)} %get-tuple-element.12.own_ref.refs_0_, f32[8,512]{1,0:T(8,128)S(1)} %far_after.1.refs_1_, f32[1,8,128]{2,1,0:T(8,128)S(1)} %collective-permute-done.3.refs_2_, f32[1,8,128]{2,1,0:T(8,128)S(1)} %collective-permute-done.4.refs_3_, ...), custom_call_target="tpu_custom_call" | custom-call | flops 2752512000 | tf_op jit(solution)/shard_map/near/pallas_call | solution.py:223
  15.9 0.0 collective-permute-done.6.refs_2_
  15.9 3.6 %far_last.1 = f32[3,512]{1,0:T(4,128)} custom-call(f32[8,512]{1,0:T(8,128)S(1)} %get-tuple-element.12.own_ref.refs_0_, f32[8,512]{1,0:T(8,128)S(1)} %near.1.refs_1_, f32[24,512]{1,0:T(8,128)S(1)} %collective-permute-done.6.refs_2_), custom_call_target="tpu_custom_call" | custom-call | flops 2752512000 | tf_op jit(solution)/shard_map/far_last/pallas_call | solution.py:223
  (5 shorter events, 0.0 us)
Async XLA Ops:
  1.8 3.7 %copy-start.1 = (s32[1,12,2]{1,2,0:T(2,128)S(1)}, s32[1,12,2]{1,2,0:T(2,128)}, u32[]{:S(2)}) copy-start(s32[1,12,2]{1,2,0:T(2,128)} %param.9) | copy-start | bytes 292
  1.8 3.7 %copy-start.2 = (s32[1,4]{1,0:T(1,128)S(1)}, s32[1,4]{1,0:T(1,128)}, u32[]{:S(2)}) copy-start(s32[1,4]{1,0:T(1,128)} %map_ref.1) | copy-start | bytes 52
  1.8 7.4 %collective-permute-start = (f32[8,512]{1,0:T(8,128)S(1)}, f32[8,512]{1,0:T(8,128)S(1)}, u32[]{:S(2)}, u32[]{:S(2)}) collective-permute-start(f32[8,512]{1,0:T(8,128)S(1)} %get-tuple-element.12.own_ref.refs_0_), channel_id=1, source_target_pairs={{0,8},{4,12},{8,0},{12,4},{16,24},{20,28},{24,16},{28,20},{1,9},{5... | collective-permute-start | bytes 49160 | tf_op jit(solution)/shard_map/ppermute | solution.py:356
  4.0 5.3 %collective-permute-start.1 = (f32[8,512]{1,0:T(8,128)S(1)}, f32[8,512]{1,0:T(8,128)S(1)}, u32[]{:S(2)}, u32[]{:S(2)}) collective-permute-start(f32[8,512]{1,0:T(8,128)S(1)} %get-tuple-element.12.own_ref.refs_0_), channel_id=1, source_target_pairs={{0,12},{4,8},{8,4},{12,0},{16,28},{20,24},{24,20},{28,16},{1,13},{... | collective-permute-start | bytes 49160 | tf_op jit(solution)/shard_map/ppermute | solution.py:356
  5.4 3.9 %collective-permute-start.2 = (f32[8,512]{1,0:T(8,128)S(1)}, f32[8,512]{1,0:T(8,128)S(1)}, u32[]{:S(2)}, u32[]{:S(2)}) collective-permute-start(f32[8,512]{1,0:T(8,128)S(1)} %get-tuple-element.12.own_ref.refs_0_), channel_id=1, source_target_pairs={{0,4},{4,0},{8,12},{12,8},{16,20},{20,16},{24,28},{28,24},{1,5},{5... | collective-permute-start | bytes 49160 | tf_op jit(solution)/shard_map/ppermute | solution.py:356
  6.3 7.2 %collective-permute-start.3 = (f32[1,8,128]{2,1,0:T(8,128)S(1)}, f32[1,8,128]{2,1,0:T(8,128)S(1)}, u32[]{:S(2)}, u32[]{:S(2)}) collective-permute-start(f32[1,8,128]{2,1,0:T(8,128)S(1)} %get-tuple-element.15), channel_id=1, source_target_pairs={{0,1},{1,0},{2,3},{3,2},{4,5},{5,4},{6,7},{7,6},{8,9},{9,8},{10,11... | collective-permute-start | bytes 12296 | tf_op jit(solution)/shard_map/ppermute | solution.py:358
  6.4 7.1 %collective-permute-start.4 = (f32[1,8,128]{2,1,0:T(8,128)S(1)}, f32[1,8,128]{2,1,0:T(8,128)S(1)}, u32[]{:S(2)}, u32[]{:S(2)}) collective-permute-start(f32[1,8,128]{2,1,0:T(8,128)S(1)} %get-tuple-element.16), channel_id=1, source_target_pairs={{0,2},{1,3},{2,0},{3,1},{4,6},{5,7},{6,4},{7,5},{8,10},{9,11},{10,... | collective-permute-start | bytes 12296 | tf_op jit(solution)/shard_map/ppermute | solution.py:358
  9.2 4.3 %collective-permute-start.5 = (f32[1,8,128]{2,1,0:T(8,128)S(1)}, f32[1,8,128]{2,1,0:T(8,128)S(1)}, u32[]{:S(2)}, u32[]{:S(2)}) collective-permute-start(f32[1,8,128]{2,1,0:T(8,128)S(1)} %get-tuple-element.17), channel_id=1, source_target_pairs={{0,3},{1,2},{2,1},{3,0},{4,7},{5,6},{6,5},{7,4},{8,11},{9,10},{10,... | collective-permute-start | bytes 12296 | tf_op jit(solution)/shard_map/ppermute | solution.py:358
  10.1 5.7 %collective-permute-start.6 = (f32[24,512]{1,0:T(8,128)S(1)}, f32[24,512]{1,0:T(8,128)S(1)}, u32[]{:S(2)}, u32[]{:S(2)}) collective-permute-start(f32[24,512]{1,0:T(8,128)S(1)} %get-tuple-element.18), channel_id=1, source_target_pairs={{0,16},{4,20},{8,24},{12,28},{16,0},{20,4},{24,8},{28,12},{1,17},{... | collective-permute-start | bytes 147464 | tf_op jit(solution)/shard_map/ppermute | solution.py:364
  11.8 1.7 %copy-start = (f32[32,128]{1,0:T(8,128)S(1)}, f32[32,128]{1,0:T(8,128)}, u32[]{:S(2)}) copy-start(f32[32,128]{1,0:T(8,128)} %refs_5_.1) | copy-start | bytes 49156

commit v3 on v2

--- a/solution.py
+++ b/solution.py
@@ -16,9 +16,10 @@
 LANES = 128
 ROWS = 8
 VMEM_LIMIT = 40 * 2**20
-WIDE = 1536
+WIDE = 2048
 USED = 6
 FIRST = 1
+AHEAD = 1
 SOON = 2
 PACK_FLOPS = 900 * 10**6
 PAIR_FLOPS = 3500
@@ -172,7 +173,7 @@
 def wide_blocks(refs):
     singles = []
     for ref in refs:
-        if ref.shape[0] == ROWS:
+        if ref.shape[0] <= ROWS:
             singles.append(ref[0:USED, :])
         else:
             singles += [ref[USED * i : USED * (i + 1), :] for i in range(ref.shape[0] // USED)]
@@ -234,9 +235,9 @@
 
 def place():
     blk = lax.axis_index("blk")
-    first = blk < FIRST
-    soon = jnp.logical_and(blk >= FIRST, blk < SOON * (lax.axis_size("blk") // 4))
-    late = jnp.logical_and(blk >= FIRST, blk >= SOON * (lax.axis_size("blk") // 4))
+    first = jnp.logical_and(blk < FIRST, lax.axis_index("nbr") < lax.axis_size("nbr") // 2)
+    soon = jnp.logical_and(jnp.logical_not(first), blk < SOON * (lax.axis_size("blk") // 4))
+    late = jnp.logical_not(jnp.logical_or(first, soon))
     return first, soon, late
 
 
@@ -252,7 +253,8 @@
 
 def first_kernel(own_ref, copy_ref, out_ref):
     first, soon, late = place()
-    copy_ref[...] = own_ref[...]
+    copy_ref[0:USED, :] = own_ref[...]
+    copy_ref[USED:, :] = jnp.zeros((ROWS - USED, own_ref.shape[1]), F32)
 
     @pl.when(first)
     def _():
@@ -271,7 +273,7 @@
 
     @pl.when(first)
     def _():
-        out_ref[...] = far_total(own_ref[0:3, :], block_refs[:1], part_ref[...])
+        out_ref[...] = far_total(own_ref[0:3, :], block_refs[:AHEAD], part_ref[...])
 
     @pl.when(soon)
     def _():
@@ -288,7 +290,7 @@
 
     @pl.when(first)
     def _():
-        out_ref[...] = far_total(own_ref[0:3, :], block_refs[1:], part_ref[...])
+        out_ref[...] = far_total(own_ref[0:3, :], block_refs[AHEAD:], part_ref[...])
 
     @pl.when(soon)
     def _():
@@ -303,7 +305,7 @@
     vmem = pl.BlockSpec(memory_space=pltpu.VMEM)
     return pl.pallas_call(
         first_kernel,
-        out_shape=[jax.ShapeDtypeStruct(own.shape, F32)] * 2,
+        out_shape=[jax.ShapeDtypeStruct((ROWS, own.shape[1]), F32)] * 2,
         in_specs=[vmem],
         out_specs=[vmem] * 2,
         compiler_params=pltpu.CompilerParams(vmem_limit_bytes=VMEM_LIMIT),
@@ -351,7 +353,7 @@
 def shards(positions, density, upsample, cell_map, near_list):
     columns = lax.axis_size("blk")
     peers = lax.axis_size("nbr")
-    own = jnp.concatenate([positions, density, jnp.zeros((2, positions.shape[1]), F32)], axis=0)
+    own = jnp.concatenate([positions, density], axis=0)
     own, part = far_first(own)
     zs = [lax.ppermute(own, "blk", flips(columns, b)) for b in ORDER]
     tiles = near_panels(own, jnp.swapaxes(near_list, 1, 2), cell_map, upsample.shape[0], peers)

time: 19.7 us -> 19.5 us (0.990)
  waiting for transfers between devices: 0.02 us -> 0.76 us
  starting transfers between devices: 8.32 us -> 7.61 us
    ppermute x3, starting transfers between devices: 2.93 us -> 2.06 us  [shards(): lax.ppermute(t, 'nbr', flips(peers, d + 1))]
    ppermute x3, waiting for transfers between devices: 0.01 us -> 0.75 us  [shards(): zs = [lax.ppermute(own, 'blk', flips(columns, b)) for b in ORDER]]
  transfers between devices with their start and end apart: 7 -> 7, of which waited for: 0 -> 2; matrix products, arithmetic and copies ran while one was open for 0% -> 0% of each run, Pallas kernels for 29% -> 30%
where the time goes in v3:
time: 19.5 us; the launch traced here: 19.3 us
  Pallas kernels  10.1 us (52%)
  starting transfers between devices  7.61 us (39%)
  waiting for transfers between devices  0.76 us (4%)
  other arithmetic  0.72 us (4%)
    pallas_call x2, Pallas kernels, pair_sums(): pl.pallas_call(functools.partial(sum_kernel, len(far), len(near), prior i...  5.89 us
    ppermute x3, starting transfers between devices, shards(): zs = [lax.ppermute(own, 'blk', flips(columns, b)) for b in ORDER]  3.77 us
    ppermute x3, starting transfers between devices, shards(): lax.ppermute(t, 'nbr', flips(peers, d + 1))  2.06 us
    ppermute x1, starting transfers between devices, shards(): got = lax.ppermute(held, 'blk', flips(columns, bit))  1.78 us
    pallas_call x1, Pallas kernels, far_after(): pl.pallas_call(after_kernel, out_shape=jax.ShapeDtypeStruct(own.shape, F3...  1.65 us
    pallas_call x1, Pallas kernels, far_before(): pl.pallas_call(before_kernel, out_shape=[jax.ShapeDtypeStruct((USED * (le...  0.91 us
    pallas_call x1, Pallas kernels, far_first(): pl.pallas_call(first_kernel, out_shape=[jax.ShapeDtypeStruct((ROWS, own.s...  0.9 us
    pallas_call x1, Pallas kernels, near_panels(): pl.pallas_call(functools.partial(pick_panels, peers, slots, panel_pts), o...  0.77 us
  transfers between devices with their start and end apart: 7, of which 2 were waited for; matrix products, arithmetic and copies ran while one was open for 0% of the time, Pallas kernels for 30%

profile of v3, /device:TPU:0, one launch (start us, length us, event | category | flops | bytes accessed | tf_op | source)
XLA Modules:
  0.0 19.3 jit_solution(4639665947748521789)
XLA Ops:
  0.0 0.7 %pad_maximum_fusion.own_ref = f32[6,512]{1,0:T(8,128)S(1)} fusion(f32[3,512]{1,0:T(4,128)} %param.6, f32[3,512]{1,0:T(4,128)} %param.5), kind=kLoop, calls=%fused_computation | loop fusion | flops 3072 | bytes 24576 | tf_op jit(solution)/shard_map/concatenate | solution.py:356
  0.7 0.9 %far_first.1 = (f32[8,512]{1,0:T(8,128)S(1)}, f32[8,512]{1,0:T(8,128)S(1)}) custom-call(f32[6,512]{1,0:T(8,128)S(1)} %pad_maximum_fusion.own_ref), custom_call_target="tpu_custom_call" | custom-call | tf_op jit(solution)/shard_map/far_first/pallas_call | solution.py:306
  1.6 2.2 %collective-permute-start = (f32[8,512]{1,0:T(8,128)S(1)}, f32[8,512]{1,0:T(8,128)S(1)}, u32[]{:S(2)}, u32[]{:S(2)}) collective-permute-start(f32[8,512]{1,0:T(8,128)S(1)} %get-tuple-element.12.own_ref.refs_0_), channel_id=1, source_target_pairs={{0,8},{4,12},{8,0},{12,4},{16,24},{20,28},{24,16},{28,20},{1,9},{5... | collective-permute-start | bytes 49160 | tf_op jit(solution)/shard_map/ppermute | solution.py:358
  3.9 1.4 %collective-permute-start.1 = (f32[8,512]{1,0:T(8,128)S(1)}, f32[8,512]{1,0:T(8,128)S(1)}, u32[]{:S(2)}, u32[]{:S(2)}) collective-permute-start(f32[8,512]{1,0:T(8,128)S(1)} %get-tuple-element.12.own_ref.refs_0_), channel_id=1, source_target_pairs={{0,12},{4,8},{8,4},{12,0},{16,28},{20,24},{24,20},{28,16},{1,13},{... | collective-permute-start | bytes 49160 | tf_op jit(solution)/shard_map/ppermute | solution.py:358
  5.3 0.1 collective-permute-start.2
  5.4 0.0 copy-done.1
  5.4 0.0 copy-done.2
  5.4 0.8 %panels.1 = (f32[1,8,128]{2,1,0:T(8,128)S(1)}, f32[1,8,128]{2,1,0:T(8,128)S(1)}, f32[1,8,128]{2,1,0:T(8,128)S(1)}) custom-call(f32[8,512]{1,0:T(8,128)S(1)} %get-tuple-element.12.own_ref.refs_0_, s32[1,2,12]{2,1,0:T(2,128)S(1)} %bitcast.1, s32[1,4]{1,0:T(1,128)S(1)} %copy-done.2), custom_call_target="tpu_custom_call" | custom-call | flops 900000000 | tf_op jit(solution)/shard_map/panels/pallas_call | solution.py:161
  6.2 0.1 collective-permute-start.3
  6.3 1.9 %collective-permute-start.4 = (f32[1,8,128]{2,1,0:T(8,128)S(1)}, f32[1,8,128]{2,1,0:T(8,128)S(1)}, u32[]{:S(2)}, u32[]{:S(2)}) collective-permute-start(f32[1,8,128]{2,1,0:T(8,128)S(1)} %get-tuple-element.16), channel_id=1, source_target_pairs={{0,2},{1,3},{2,0},{3,1},{4,6},{5,7},{6,4},{7,5},{8,10},{9,11},{10,... | collective-permute-start | bytes 12296 | tf_op jit(solution)/shard_map/ppermute | solution.py:360
  8.2 0.0 collective-permute-done.refs_0_
  8.2 0.1 collective-permute-start.5
  8.3 0.2 %collective-permute-done.1.refs_1_ = f32[8,512]{1,0:T(8,128)S(1)} collective-permute-done((f32[8,512]{1,0:T(8,128)S(1)}, f32[8,512]{1,0:T(8,128)S(1)}, u32[]{:S(2)}, u32[]{:S(2)}) %collective-permute-start.1) | collective-permute-done | bytes 16416 | tf_op jit(solution)/shard_map/ppermute | solution.py:358
  8.5 0.5 %collective-permute-done.2.refs_2_ = f32[8,512]{1,0:T(8,128)S(1)} collective-permute-done((f32[8,512]{1,0:T(8,128)S(1)}, f32[8,512]{1,0:T(8,128)S(1)}, u32[]{:S(2)}, u32[]{:S(2)}) %collective-permute-start.2) | collective-permute-done | bytes 16416 | tf_op jit(solution)/shard_map/ppermute | solution.py:358
  9.0 0.9 %far_before.1 = (f32[24,512]{1,0:T(8,128)S(1)}, f32[8,512]{1,0:T(8,128)S(1)}) custom-call(f32[8,512]{1,0:T(8,128)S(1)} %get-tuple-element.12.own_ref.refs_0_, f32[8,512]{1,0:T(8,128)S(1)} %get-tuple-element.13.part_ref, f32[8,512]{1,0:T(8,128)S(1)} %collective-permute-done.refs_0_, f32[8,512]{1,0:T(8,128)S(1)} %collective-permute-done.1.refs_1_, ...), custom_call_target="tpu_custom_call" | custom-call | tf_op jit(solution)/shard_map/far_before/pallas_call | solution.py:318
  9.9 1.8 %collective-permute-start.6 = (f32[24,512]{1,0:T(8,128)S(1)}, f32[24,512]{1,0:T(8,128)S(1)}, u32[]{:S(2)}, u32[]{:S(2)}) collective-permute-start(f32[24,512]{1,0:T(8,128)S(1)} %get-tuple-element.18), channel_id=1, source_target_pairs={{0,16},{4,20},{8,24},{12,28},{16,0},{20,4},{24,8},{28,12},{1,17},{... | collective-permute-start | bytes 147464 | tf_op jit(solution)/shard_map/ppermute | solution.py:366
  11.7 1.6 %far_after.1.refs_1_ = f32[8,512]{1,0:T(8,128)S(1)} custom-call(f32[8,512]{1,0:T(8,128)S(1)} %get-tuple-element.12.own_ref.refs_0_, f32[8,512]{1,0:T(8,128)S(1)} %get-tuple-element.14.part_ref, f32[8,512]{1,0:T(8,128)S(1)} %collective-permute-done.refs_0_, f32[8,512]{1,0:T(8,128)S(1)} %collective-permute-done.1.refs_1_, ...), custom_call_target="tpu_custom_call" | custom-call | flops 3670016000 | tf_op jit(solution)/shard_map/far_after/pallas_call | solution.py:334
  13.3 0.0 collective-permute-done.3.refs_2_
  13.4 0.0 collective-permute-done.4.refs_3_
  13.4 0.0 collective-permute-done.5.refs_4_
  13.4 0.0 copy-done
  13.4 2.4 %near.1.refs_1_ = f32[8,512]{1,0:T(8,128)S(1)} custom-call(f32[8,512]{1,0:T(8,128)S(1)} %get-tuple-element.12.own_ref.refs_0_, f32[8,512]{1,0:T(8,128)S(1)} %far_after.1.refs_1_, f32[1,8,128]{2,1,0:T(8,128)S(1)} %collective-permute-done.3.refs_2_, f32[1,8,128]{2,1,0:T(8,128)S(1)} %collective-permute-done.4.refs_3_, ...), custom_call_target="tpu_custom_call" | custom-call | flops 2752512000 | tf_op jit(solution)/shard_map/near/pallas_call | solution.py:224
  15.8 0.0 collective-permute-done.6.refs_2_
  15.8 3.5 %far_last.1 = f32[3,512]{1,0:T(4,128)} custom-call(f32[8,512]{1,0:T(8,128)S(1)} %get-tuple-element.12.own_ref.refs_0_, f32[8,512]{1,0:T(8,128)S(1)} %near.1.refs_1_, f32[24,512]{1,0:T(8,128)S(1)} %collective-permute-done.6.refs_2_), custom_call_target="tpu_custom_call" | custom-call | flops 2752512000 | tf_op jit(solution)/shard_map/far_last/pallas_call | solution.py:224
  (3 shorter events, 0.0 us)
Async XLA Ops:
  1.6 3.8 %copy-start.1 = (s32[1,12,2]{1,2,0:T(2,128)S(1)}, s32[1,12,2]{1,2,0:T(2,128)}, u32[]{:S(2)}) copy-start(s32[1,12,2]{1,2,0:T(2,128)} %param.9) | copy-start | bytes 292
  1.6 3.8 %copy-start.2 = (s32[1,4]{1,0:T(1,128)S(1)}, s32[1,4]{1,0:T(1,128)}, u32[]{:S(2)}) copy-start(s32[1,4]{1,0:T(1,128)} %map_ref.1) | copy-start | bytes 52
  1.6 6.6 %collective-permute-start = (f32[8,512]{1,0:T(8,128)S(1)}, f32[8,512]{1,0:T(8,128)S(1)}, u32[]{:S(2)}, u32[]{:S(2)}) collective-permute-start(f32[8,512]{1,0:T(8,128)S(1)} %get-tuple-element.12.own_ref.refs_0_), channel_id=1, source_target_pairs={{0,8},{4,12},{8,0},{12,4},{16,24},{20,28},{24,16},{28,20},{1,9},{5... | collective-permute-start | bytes 49160 | tf_op jit(solution)/shard_map/ppermute | solution.py:358
  3.9 4.6 %collective-permute-start.1 = (f32[8,512]{1,0:T(8,128)S(1)}, f32[8,512]{1,0:T(8,128)S(1)}, u32[]{:S(2)}, u32[]{:S(2)}) collective-permute-start(f32[8,512]{1,0:T(8,128)S(1)} %get-tuple-element.12.own_ref.refs_0_), channel_id=1, source_target_pairs={{0,12},{4,8},{8,4},{12,0},{16,28},{20,24},{24,20},{28,16},{1,13},{... | collective-permute-start | bytes 49160 | tf_op jit(solution)/shard_map/ppermute | solution.py:358
  5.3 3.7 %collective-permute-start.2 = (f32[8,512]{1,0:T(8,128)S(1)}, f32[8,512]{1,0:T(8,128)S(1)}, u32[]{:S(2)}, u32[]{:S(2)}) collective-permute-start(f32[8,512]{1,0:T(8,128)S(1)} %get-tuple-element.12.own_ref.refs_0_), channel_id=1, source_target_pairs={{0,4},{4,0},{8,12},{12,8},{16,20},{20,16},{24,28},{28,24},{1,5},{5... | collective-permute-start | bytes 49160 | tf_op jit(solution)/shard_map/ppermute | solution.py:358
  6.2 7.2 %collective-permute-start.3 = (f32[1,8,128]{2,1,0:T(8,128)S(1)}, f32[1,8,128]{2,1,0:T(8,128)S(1)}, u32[]{:S(2)}, u32[]{:S(2)}) collective-permute-start(f32[1,8,128]{2,1,0:T(8,128)S(1)} %get-tuple-element.15), channel_id=1, source_target_pairs={{0,1},{1,0},{2,3},{3,2},{4,5},{5,4},{6,7},{7,6},{8,9},{9,8},{10,11... | collective-permute-start | bytes 12296 | tf_op jit(solution)/shard_map/ppermute | solution.py:360
  6.3 7.1 %collective-permute-start.4 = (f32[1,8,128]{2,1,0:T(8,128)S(1)}, f32[1,8,128]{2,1,0:T(8,128)S(1)}, u32[]{:S(2)}, u32[]{:S(2)}) collective-permute-start(f32[1,8,128]{2,1,0:T(8,128)S(1)} %get-tuple-element.16), channel_id=1, source_target_pairs={{0,2},{1,3},{2,0},{3,1},{4,6},{5,7},{6,4},{7,5},{8,10},{9,11},{10,... | collective-permute-start | bytes 12296 | tf_op jit(solution)/shard_map/ppermute | solution.py:360
  8.2 5.2 %collective-permute-start.5 = (f32[1,8,128]{2,1,0:T(8,128)S(1)}, f32[1,8,128]{2,1,0:T(8,128)S(1)}, u32[]{:S(2)}, u32[]{:S(2)}) collective-permute-start(f32[1,8,128]{2,1,0:T(8,128)S(1)} %get-tuple-element.17), channel_id=1, source_target_pairs={{0,3},{1,2},{2,1},{3,0},{4,7},{5,6},{6,5},{7,4},{8,11},{9,10},{10,... | collective-permute-start | bytes 12296 | tf_op jit(solution)/shard_map/ppermute | solution.py:360
  9.9 5.9 %collective-permute-start.6 = (f32[24,512]{1,0:T(8,128)S(1)}, f32[24,512]{1,0:T(8,128)S(1)}, u32[]{:S(2)}, u32[]{:S(2)}) collective-permute-start(f32[24,512]{1,0:T(8,128)S(1)} %get-tuple-element.18), channel_id=1, source_target_pairs={{0,16},{4,20},{8,24},{12,28},{16,0},{20,4},{24,8},{28,12},{1,17},{... | collective-permute-start | bytes 147464 | tf_op jit(solution)/shard_map/ppermute | solution.py:366
  11.7 1.7 %copy-start = (f32[32,128]{1,0:T(8,128)S(1)}, f32[32,128]{1,0:T(8,128)}, u32[]{:S(2)}) copy-start(f32[32,128]{1,0:T(8,128)} %refs_5_.1) | copy-start | bytes 49156

commit v4 on v3

--- a/solution.py
+++ b/solution.py
@@ -19,7 +19,6 @@
 WIDE = 2048
 USED = 6
 FIRST = 1
-AHEAD = 1
 SOON = 2
 PACK_FLOPS = 900 * 10**6
 PAIR_FLOPS = 3500
@@ -233,6 +232,19 @@
     return got[0]
 
 
+NEEDS = 2
+
+
+def ahead_of(blocks):
+    half = blocks[1].shape[1] // 4
+    return [blocks[0], blocks[1].at[:, 0:half]]
+
+
+def rest_of(blocks):
+    half = blocks[1].shape[1] // 4
+    return [blocks[1].at[:, half:], *blocks[2:]]
+
+
 def place():
     blk = lax.axis_index("blk")
     first = jnp.logical_and(blk < FIRST, lax.axis_index("nbr") < lax.axis_size("nbr") // 2)
@@ -265,23 +277,27 @@
         out_ref[...] = jnp.zeros(out_ref.shape, F32)
 
 
-def before_kernel(own_ref, part_ref, *refs):
-    *block_refs, held_ref, out_ref = refs
+def ahead_kernel(own_ref, part_ref, *refs):
+    *block_refs, out_ref = refs
     first, soon, late = place()
+
+    @pl.when(first)
+    def _():
+        out_ref[...] = far_total(own_ref[0:3, :], ahead_of(block_refs), part_ref[...])
+
+    @pl.when(soon)
+    def _():
+        out_ref[...] = far_total(own_ref[0:3, :], [own_ref], part_ref[...])
+
+    @pl.when(late)
+    def _():
+        out_ref[...] = part_ref[...]
+
+
+def stack_kernel(own_ref, after_ref, *refs):
+    *block_refs, held_ref = refs
     for i, ref in enumerate([own_ref, *block_refs]):
         held_ref[USED * i : USED * (i + 1), :] = ref[0:USED, :]
-
-    @pl.when(first)
-    def _():
-        out_ref[...] = far_total(own_ref[0:3, :], block_refs[:AHEAD], part_ref[...])
-
-    @pl.when(soon)
-    def _():
-        out_ref[...] = far_total(own_ref[0:3, :], [own_ref], part_ref[...])
-
-    @pl.when(late)
-    def _():
-        out_ref[...] = part_ref[...]
 
 
 def after_kernel(own_ref, part_ref, *refs):
@@ -290,7 +306,7 @@
 
     @pl.when(first)
     def _():
-        out_ref[...] = far_total(own_ref[0:3, :], block_refs[AHEAD:], part_ref[...])
+        out_ref[...] = far_total(own_ref[0:3, :], rest_of(block_refs), part_ref[...])
 
     @pl.when(soon)
     def _():
@@ -313,19 +329,30 @@
     )(own)
 
 
-def far_before(own, part, blocks):
-    vmem = pl.BlockSpec(memory_space=pltpu.VMEM)
+def far_ahead(own, part, blocks):
+    vmem = pl.BlockSpec(memory_space=pltpu.VMEM)
+    pairs = own.shape[1] ** 2
     return pl.pallas_call(
-        before_kernel,
-        out_shape=[
-            jax.ShapeDtypeStruct((USED * (len(blocks) + 1), own.shape[1]), F32),
-            jax.ShapeDtypeStruct(own.shape, F32),
-        ],
+        ahead_kernel,
+        out_shape=jax.ShapeDtypeStruct(own.shape, F32),
         in_specs=[vmem] * (2 + len(blocks)),
-        out_specs=[vmem] * 2,
-        compiler_params=pltpu.CompilerParams(vmem_limit_bytes=VMEM_LIMIT),
-        name="far_before",
+        out_specs=vmem,
+        compiler_params=pltpu.CompilerParams(vmem_limit_bytes=VMEM_LIMIT),
+        cost_estimate=pl.CostEstimate(flops=PAIR_FLOPS * pairs, bytes_accessed=0, transcendentals=pairs),
+        name="far_ahead",
     )(own, part, *blocks)
+
+
+def stack(own, after, blocks):
+    vmem = pl.BlockSpec(memory_space=pltpu.VMEM)
+    return pl.pallas_call(
+        stack_kernel,
+        out_shape=jax.ShapeDtypeStruct((USED * (len(blocks) + 1), own.shape[1]), F32),
+        in_specs=[vmem, pl.BlockSpec(memory_space=pl.ANY)] + [vmem] * len(blocks),
+        out_specs=vmem,
+        compiler_params=pltpu.CompilerParams(vmem_limit_bytes=VMEM_LIMIT),
+        name="stack",
+    )(own, after, *blocks)
 
 
 def far_after(own, part, blocks):
@@ -358,7 +385,8 @@
     zs = [lax.ppermute(own, "blk", flips(columns, b)) for b in ORDER]
     tiles = near_panels(own, jnp.swapaxes(near_list, 1, 2), cell_map, upsample.shape[0], peers)
     near = [lax.ppermute(t, "nbr", flips(peers, d + 1)) for d, t in enumerate(tiles)]
-    held, part = far_before(own, part, zs)
+    part = far_ahead(own, part, zs[:NEEDS])
+    held = stack(own, part, zs)
     last = None
     for bit in LATER:
         if bit >= columns:

time: 19.5 us -> 19.5 us (level)
  waiting for transfers between devices: 0.76 us -> 0.38 us
  starting transfers between devices: 7.61 us -> 7.9 us
    ppermute x3, waiting for transfers between devices: 0.75 us -> 0.25 us  [shards(): zs = [lax.ppermute(own, 'blk', flips(columns, b)) for b in ORDER]]
    ppermute x1, starting transfers between devices: 1.78 us -> 2.07 us  [shards(): got = lax.ppermute(held, 'blk', flips(columns, bit))]
    pallas_call x1 -> x2, Pallas kernels: 0.91 us -> 1.1 us  [the longest x1 1.08 us: far_ahead(): pl.pallas_call(ahead_kernel, out_shape=jax.ShapeDtypeStruct(own.shape, F3...]
where the time goes in v4:
time: 19.5 us; the launch traced here: 19.2 us
  Pallas kernels  10.1 us (52%)
  starting transfers between devices  7.9 us (41%)
  other arithmetic  0.72 us (4%)
  waiting for transfers between devices  0.38 us (2%)
    pallas_call x2, Pallas kernels, pair_sums(): pl.pallas_call(functools.partial(sum_kernel, len(far), len(near), prior i...  5.88 us
    ppermute x3, starting transfers between devices, shards(): zs = [lax.ppermute(own, 'blk', flips(columns, b)) for b in ORDER]  3.77 us
    ppermute x1, starting transfers between devices, shards(): got = lax.ppermute(held, 'blk', flips(columns, bit))  2.07 us
    ppermute x3, starting transfers between devices, shards(): lax.ppermute(t, 'nbr', flips(peers, d + 1))  2.06 us
    pallas_call x1, Pallas kernels, far_after(): pl.pallas_call(after_kernel, out_shape=jax.ShapeDtypeStruct(own.shape, F3...  1.47 us
    pallas_call x1, Pallas kernels, far_ahead(): pl.pallas_call(ahead_kernel, out_shape=jax.ShapeDtypeStruct(own.shape, F3...  1.08 us
    pallas_call x1, Pallas kernels, far_first(): pl.pallas_call(first_kernel, out_shape=[jax.ShapeDtypeStruct((ROWS, own.s...  0.9 us
    pallas_call x1, Pallas kernels, near_panels(): pl.pallas_call(functools.partial(pick_panels, peers, slots, panel_pts), o...  0.77 us
  transfers between devices with their start and end apart: 7, of which 2 were waited for; matrix products, arithmetic and copies ran while one was open for 0% of the time, Pallas kernels for 30%

profile of v4, /device:TPU:0, one launch (start us, length us, event | category | flops | bytes accessed | tf_op | source)
XLA Modules:
  0.0 19.2 jit_solution(1636899512967923548)
XLA Ops:
  0.0 0.7 %pad_maximum_fusion.own_ref = f32[6,512]{1,0:T(8,128)S(1)} fusion(f32[3,512]{1,0:T(4,128)} %param.6, f32[3,512]{1,0:T(4,128)} %param.5), kind=kLoop, calls=%fused_computation | loop fusion | flops 3072 | bytes 24576 | tf_op jit(solution)/shard_map/concatenate | solution.py:383
  0.7 0.9 %far_first.1 = (f32[8,512]{1,0:T(8,128)S(1)}, f32[8,512]{1,0:T(8,128)S(1)}) custom-call(f32[6,512]{1,0:T(8,128)S(1)} %pad_maximum_fusion.own_ref), custom_call_target="tpu_custom_call" | custom-call | tf_op jit(solution)/shard_map/far_first/pallas_call | solution.py:322
  1.6 2.2 %collective-permute-start = (f32[8,512]{1,0:T(8,128)S(1)}, f32[8,512]{1,0:T(8,128)S(1)}, u32[]{:S(2)}, u32[]{:S(2)}) collective-permute-start(f32[8,512]{1,0:T(8,128)S(1)} %get-tuple-element.10.own_ref.refs_0_), channel_id=1, source_target_pairs={{0,8},{4,12},{8,0},{12,4},{16,24},{20,28},{24,16},{28,20},{1,9},{5... | collective-permute-start | bytes 49160 | tf_op jit(solution)/shard_map/ppermute | solution.py:385
  3.9 1.4 %collective-permute-start.1 = (f32[8,512]{1,0:T(8,128)S(1)}, f32[8,512]{1,0:T(8,128)S(1)}, u32[]{:S(2)}, u32[]{:S(2)}) collective-permute-start(f32[8,512]{1,0:T(8,128)S(1)} %get-tuple-element.10.own_ref.refs_0_), channel_id=1, source_target_pairs={{0,12},{4,8},{8,4},{12,0},{16,28},{20,24},{24,20},{28,16},{1,13},{... | collective-permute-start | bytes 49160 | tf_op jit(solution)/shard_map/ppermute | solution.py:385
  5.3 0.1 collective-permute-start.2
  5.4 0.0 copy-done.1
  5.4 0.8 %panels.1 = (f32[1,8,128]{2,1,0:T(8,128)S(1)}, f32[1,8,128]{2,1,0:T(8,128)S(1)}, f32[1,8,128]{2,1,0:T(8,128)S(1)}) custom-call(f32[8,512]{1,0:T(8,128)S(1)} %get-tuple-element.10.own_ref.refs_0_, s32[1,2,12]{2,1,0:T(2,128)S(1)} %bitcast.1, s32[1,4]{1,0:T(1,128)S(1)} %copy-done.2), custom_call_target="tpu_custom_call" | custom-call | flops 900000000 | tf_op jit(solution)/shard_map/panels/pallas_call | solution.py:160
  6.2 0.1 collective-permute-start.3
  6.3 1.9 %collective-permute-start.4 = (f32[1,8,128]{2,1,0:T(8,128)S(1)}, f32[1,8,128]{2,1,0:T(8,128)S(1)}, u32[]{:S(2)}, u32[]{:S(2)}) collective-permute-start(f32[1,8,128]{2,1,0:T(8,128)S(1)} %get-tuple-element.13), channel_id=1, source_target_pairs={{0,2},{1,3},{2,0},{3,1},{4,6},{5,7},{6,4},{7,5},{8,10},{9,11},{10,... | collective-permute-start | bytes 12296 | tf_op jit(solution)/shard_map/ppermute | solution.py:387
  8.2 0.0 collective-permute-done.refs_0_
  8.2 0.1 collective-permute-start.5
  8.3 0.2 %collective-permute-done.1.refs_1_ = f32[8,512]{1,0:T(8,128)S(1)} collective-permute-done((f32[8,512]{1,0:T(8,128)S(1)}, f32[8,512]{1,0:T(8,128)S(1)}, u32[]{:S(2)}, u32[]{:S(2)}) %collective-permute-start.1) | collective-permute-done | bytes 16416 | tf_op jit(solution)/shard_map/ppermute | solution.py:385
  8.5 1.1 %far_ahead.1.part_ref.after_ref = f32[8,512]{1,0:T(8,128)S(1)} custom-call(f32[8,512]{1,0:T(8,128)S(1)} %get-tuple-element.10.own_ref.refs_0_, f32[8,512]{1,0:T(8,128)S(1)} %get-tuple-element.11.part_ref, f32[8,512]{1,0:T(8,128)S(1)} %collective-permute-done.refs_0_, f32[8,512]{1,0:T(8,128)S(1)} %collective-permute-done.1.refs_1_), custom_call_target="tpu_custom_call" | custom-call | flops 917504000 | tf_op jit(solution)/shard_map/far_ahead/pallas_call | solution.py:335
  9.6 0.0 collective-permute-done.2.refs_2_
  9.6 0.0 copy-start
  9.6 2.1 %collective-permute-start.6 = (f32[24,512]{1,0:T(8,128)S(1)}, f32[24,512]{1,0:T(8,128)S(1)}, u32[]{:S(2)}, u32[]{:S(2)}) collective-permute-start(f32[24,512]{1,0:T(8,128)S(1)} %stack.1), channel_id=1, source_target_pairs={{0,16},{4,20},{8,24},{12,28},{16,0},{20,4},{24,8},{28,12},{1,17},{... | collective-permute-start | bytes 147464 | tf_op jit(solution)/shard_map/ppermute | solution.py:394
  11.7 1.5 %far_after.1.refs_1_ = f32[8,512]{1,0:T(8,128)S(1)} custom-call(f32[8,512]{1,0:T(8,128)S(1)} %get-tuple-element.10.own_ref.refs_0_, f32[8,512]{1,0:T(8,128)S(1)} %far_ahead.1.part_ref.after_ref, f32[8,512]{1,0:T(8,128)S(1)} %collective-permute-done.refs_0_, f32[8,512]{1,0:T(8,128)S(1)} %collective-permute-done.1.refs_1_, ...), custom_call_target="tpu_custom_call" | custom-call | flops 3670016000 | tf_op jit(solution)/shard_map/far_after/pallas_call | solution.py:361
  13.2 0.0 collective-permute-done.3.refs_2_
  13.2 0.0 collective-permute-done.4.refs_3_
  13.2 0.0 collective-permute-done.5.refs_4_
  13.2 0.0 copy-done
  13.2 2.4 %near.1.refs_1_ = f32[8,512]{1,0:T(8,128)S(1)} custom-call(f32[8,512]{1,0:T(8,128)S(1)} %get-tuple-element.10.own_ref.refs_0_, f32[8,512]{1,0:T(8,128)S(1)} %far_after.1.refs_1_, f32[1,8,128]{2,1,0:T(8,128)S(1)} %collective-permute-done.3.refs_2_, f32[1,8,128]{2,1,0:T(8,128)S(1)} %collective-permute-done.4.refs_3_, ...), custom_call_target="tpu_custom_call" | custom-call | flops 2752512000 | tf_op jit(solution)/shard_map/near/pallas_call | solution.py:223
  15.6 0.1 collective-permute-done.6.refs_2_
  15.7 3.5 %far_last.1 = f32[3,512]{1,0:T(4,128)} custom-call(f32[8,512]{1,0:T(8,128)S(1)} %get-tuple-element.10.own_ref.refs_0_, f32[8,512]{1,0:T(8,128)S(1)} %near.1.refs_1_, f32[24,512]{1,0:T(8,128)S(1)} %collective-permute-done.6.refs_2_), custom_call_target="tpu_custom_call" | custom-call | flops 2752512000 | tf_op jit(solution)/shard_map/far_last/pallas_call | solution.py:223
  (4 shorter events, 0.0 us)
Async XLA Ops:
  1.6 3.8 %copy-start.1 = (s32[1,12,2]{1,2,0:T(2,128)S(1)}, s32[1,12,2]{1,2,0:T(2,128)}, u32[]{:S(2)}) copy-start(s32[1,12,2]{1,2,0:T(2,128)} %param.9) | copy-start | bytes 292
  1.6 3.8 %copy-start.2 = (s32[1,4]{1,0:T(1,128)S(1)}, s32[1,4]{1,0:T(1,128)}, u32[]{:S(2)}) copy-start(s32[1,4]{1,0:T(1,128)} %map_ref.1) | copy-start | bytes 52
  1.6 6.6 %collective-permute-start = (f32[8,512]{1,0:T(8,128)S(1)}, f32[8,512]{1,0:T(8,128)S(1)}, u32[]{:S(2)}, u32[]{:S(2)}) collective-permute-start(f32[8,512]{1,0:T(8,128)S(1)} %get-tuple-element.10.own_ref.refs_0_), channel_id=1, source_target_pairs={{0,8},{4,12},{8,0},{12,4},{16,24},{20,28},{24,16},{28,20},{1,9},{5... | collective-permute-start | bytes 49160 | tf_op jit(solution)/shard_map/ppermute | solution.py:385
  3.9 4.6 %collective-permute-start.1 = (f32[8,512]{1,0:T(8,128)S(1)}, f32[8,512]{1,0:T(8,128)S(1)}, u32[]{:S(2)}, u32[]{:S(2)}) collective-permute-start(f32[8,512]{1,0:T(8,128)S(1)} %get-tuple-element.10.own_ref.refs_0_), channel_id=1, source_target_pairs={{0,12},{4,8},{8,4},{12,0},{16,28},{20,24},{24,20},{28,16},{1,13},{... | collective-permute-start | bytes 49160 | tf_op jit(solution)/shard_map/ppermute | solution.py:385
  5.3 4.3 %collective-permute-start.2 = (f32[8,512]{1,0:T(8,128)S(1)}, f32[8,512]{1,0:T(8,128)S(1)}, u32[]{:S(2)}, u32[]{:S(2)}) collective-permute-start(f32[8,512]{1,0:T(8,128)S(1)} %get-tuple-element.10.own_ref.refs_0_), channel_id=1, source_target_pairs={{0,4},{4,0},{8,12},{12,8},{16,20},{20,16},{24,28},{28,24},{1,5},{5... | collective-permute-start | bytes 49160 | tf_op jit(solution)/shard_map/ppermute | solution.py:385
  6.2 7.0 %collective-permute-start.3 = (f32[1,8,128]{2,1,0:T(8,128)S(1)}, f32[1,8,128]{2,1,0:T(8,128)S(1)}, u32[]{:S(2)}, u32[]{:S(2)}) collective-permute-start(f32[1,8,128]{2,1,0:T(8,128)S(1)} %get-tuple-element.12), channel_id=1, source_target_pairs={{0,1},{1,0},{2,3},{3,2},{4,5},{5,4},{6,7},{7,6},{8,9},{9,8},{10,11... | collective-permute-start | bytes 12296 | tf_op jit(solution)/shard_map/ppermute | solution.py:387
  6.3 6.9 %collective-permute-start.4 = (f32[1,8,128]{2,1,0:T(8,128)S(1)}, f32[1,8,128]{2,1,0:T(8,128)S(1)}, u32[]{:S(2)}, u32[]{:S(2)}) collective-permute-start(f32[1,8,128]{2,1,0:T(8,128)S(1)} %get-tuple-element.13), channel_id=1, source_target_pairs={{0,2},{1,3},{2,0},{3,1},{4,6},{5,7},{6,4},{7,5},{8,10},{9,11},{10,... | collective-permute-start | bytes 12296 | tf_op jit(solution)/shard_map/ppermute | solution.py:387
  8.2 5.0 %collective-permute-start.5 = (f32[1,8,128]{2,1,0:T(8,128)S(1)}, f32[1,8,128]{2,1,0:T(8,128)S(1)}, u32[]{:S(2)}, u32[]{:S(2)}) collective-permute-start(f32[1,8,128]{2,1,0:T(8,128)S(1)} %get-tuple-element.14), channel_id=1, source_target_pairs={{0,3},{1,2},{2,1},{3,0},{4,7},{5,6},{6,5},{7,4},{8,11},{9,10},{10,... | collective-permute-start | bytes 12296 | tf_op jit(solution)/shard_map/ppermute | solution.py:387
  9.6 3.6 %copy-start = (f32[32,128]{1,0:T(8,128)S(1)}, f32[32,128]{1,0:T(8,128)}, u32[]{:S(2)}) copy-start(f32[32,128]{1,0:T(8,128)} %refs_5_.1) | copy-start | bytes 49156
  9.6 6.1 %collective-permute-start.6 = (f32[24,512]{1,0:T(8,128)S(1)}, f32[24,512]{1,0:T(8,128)S(1)}, u32[]{:S(2)}, u32[]{:S(2)}) collective-permute-start(f32[24,512]{1,0:T(8,128)S(1)} %stack.1), channel_id=1, source_target_pairs={{0,16},{4,20},{8,24},{12,28},{16,0},{20,4},{24,8},{28,12},{1,17},{... | collective-permute-start | bytes 147464 | tf_op jit(solution)/shard_map/ppermute | solution.py:394

commit v5 on v4

--- a/solution.py
+++ b/solution.py
@@ -19,7 +19,7 @@
 WIDE = 2048
 USED = 6
 FIRST = 1
-SOON = 2
+SOON = 1
 PACK_FLOPS = 900 * 10**6
 PAIR_FLOPS = 3500
 

time: 19.5 us -> 19.4 us (level)
  transfers between devices with their start and end apart: 7 -> 7, of which waited for: 2 -> 1; matrix products, arithmetic and copies ran while one was open for 0% -> 0% of each run, Pallas kernels for 30% -> 30%
where the time goes in v5:
time: 19.4 us; the launch traced here: 19.1 us
  Pallas kernels  10.1 us (52%)
  starting transfers between devices  7.9 us (41%)
  other arithmetic  0.72 us (4%)
  waiting for transfers between devices  0.26 us (1%)
    pallas_call x2, Pallas kernels, pair_sums(): pl.pallas_call(functools.partial(sum_kernel, len(far), len(near), prior i...  5.89 us
    ppermute x3, starting transfers between devices, shards(): zs = [lax.ppermute(own, 'blk', flips(columns, b)) for b in ORDER]  3.77 us
    ppermute x1, starting transfers between devices, shards(): got = lax.ppermute(held, 'blk', flips(columns, bit))  2.07 us
    ppermute x3, starting transfers between devices, shards(): lax.ppermute(t, 'nbr', flips(peers, d + 1))  2.06 us
    pallas_call x1, Pallas kernels, far_after(): pl.pallas_call(after_kernel, out_shape=jax.ShapeDtypeStruct(own.shape, F3...  1.47 us
    pallas_call x1, Pallas kernels, far_ahead(): pl.pallas_call(ahead_kernel, out_shape=jax.ShapeDtypeStruct(own.shape, F3...  1.08 us
    pallas_call x1, Pallas kernels, far_first(): pl.pallas_call(first_kernel, out_shape=[jax.ShapeDtypeStruct((ROWS, own.s...  0.9 us
    pallas_call x1, Pallas kernels, near_panels(): pl.pallas_call(functools.partial(pick_panels, peers, slots, panel_pts), o...  0.77 us
  transfers between devices with their start and end apart: 7, of which 1 were waited for; matrix products, arithmetic and copies ran while one was open for 0% of the time, Pallas kernels for 30%

profile of v5, /device:TPU:0, one launch (start us, length us, event | category | flops | bytes accessed | tf_op | source)
XLA Modules:
  0.0 19.1 jit_solution(6988286370017592724)
XLA Ops:
  0.0 0.7 %pad_maximum_fusion.own_ref = f32[6,512]{1,0:T(8,128)S(1)} fusion(f32[3,512]{1,0:T(4,128)} %param.6, f32[3,512]{1,0:T(4,128)} %param.5), kind=kLoop, calls=%fused_computation | loop fusion | flops 3072 | bytes 24576 | tf_op jit(solution)/shard_map/concatenate | solution.py:383
  0.7 0.9 %far_first.1 = (f32[8,512]{1,0:T(8,128)S(1)}, f32[8,512]{1,0:T(8,128)S(1)}) custom-call(f32[6,512]{1,0:T(8,128)S(1)} %pad_maximum_fusion.own_ref), custom_call_target="tpu_custom_call" | custom-call | tf_op jit(solution)/shard_map/far_first/pallas_call | solution.py:322
  1.6 2.2 %collective-permute-start = (f32[8,512]{1,0:T(8,128)S(1)}, f32[8,512]{1,0:T(8,128)S(1)}, u32[]{:S(2)}, u32[]{:S(2)}) collective-permute-start(f32[8,512]{1,0:T(8,128)S(1)} %get-tuple-element.10.own_ref.refs_0_), channel_id=1, source_target_pairs={{0,8},{4,12},{8,0},{12,4},{16,24},{20,28},{24,16},{28,20},{1,9},{5... | collective-permute-start | bytes 49160 | tf_op jit(solution)/shard_map/ppermute | solution.py:385
  3.9 1.4 %collective-permute-start.1 = (f32[8,512]{1,0:T(8,128)S(1)}, f32[8,512]{1,0:T(8,128)S(1)}, u32[]{:S(2)}, u32[]{:S(2)}) collective-permute-start(f32[8,512]{1,0:T(8,128)S(1)} %get-tuple-element.10.own_ref.refs_0_), channel_id=1, source_target_pairs={{0,12},{4,8},{8,4},{12,0},{16,28},{20,24},{24,20},{28,16},{1,13},{... | collective-permute-start | bytes 49160 | tf_op jit(solution)/shard_map/ppermute | solution.py:385
  5.3 0.1 collective-permute-start.2
  5.4 0.0 copy-done.1
  5.4 0.8 %panels.1 = (f32[1,8,128]{2,1,0:T(8,128)S(1)}, f32[1,8,128]{2,1,0:T(8,128)S(1)}, f32[1,8,128]{2,1,0:T(8,128)S(1)}) custom-call(f32[8,512]{1,0:T(8,128)S(1)} %get-tuple-element.10.own_ref.refs_0_, s32[1,2,12]{2,1,0:T(2,128)S(1)} %bitcast.1, s32[1,4]{1,0:T(1,128)S(1)} %copy-done.2), custom_call_target="tpu_custom_call" | custom-call | flops 900000000 | tf_op jit(solution)/shard_map/panels/pallas_call | solution.py:160
  6.2 0.1 collective-permute-start.3
  6.3 1.9 %collective-permute-start.4 = (f32[1,8,128]{2,1,0:T(8,128)S(1)}, f32[1,8,128]{2,1,0:T(8,128)S(1)}, u32[]{:S(2)}, u32[]{:S(2)}) collective-permute-start(f32[1,8,128]{2,1,0:T(8,128)S(1)} %get-tuple-element.13), channel_id=1, source_target_pairs={{0,2},{1,3},{2,0},{3,1},{4,6},{5,7},{6,4},{7,5},{8,10},{9,11},{10,... | collective-permute-start | bytes 12296 | tf_op jit(solution)/shard_map/ppermute | solution.py:387
  8.2 0.0 collective-permute-done.refs_0_
  8.2 0.1 collective-permute-start.5
  8.3 0.2 %collective-permute-done.1.refs_1_ = f32[8,512]{1,0:T(8,128)S(1)} collective-permute-done((f32[8,512]{1,0:T(8,128)S(1)}, f32[8,512]{1,0:T(8,128)S(1)}, u32[]{:S(2)}, u32[]{:S(2)}) %collective-permute-start.1) | collective-permute-done | bytes 16416 | tf_op jit(solution)/shard_map/ppermute | solution.py:385
  8.5 1.1 %far_ahead.1.part_ref.after_ref = f32[8,512]{1,0:T(8,128)S(1)} custom-call(f32[8,512]{1,0:T(8,128)S(1)} %get-tuple-element.10.own_ref.refs_0_, f32[8,512]{1,0:T(8,128)S(1)} %get-tuple-element.11.part_ref, f32[8,512]{1,0:T(8,128)S(1)} %collective-permute-done.refs_0_, f32[8,512]{1,0:T(8,128)S(1)} %collective-permute-done.1.refs_1_), custom_call_target="tpu_custom_call" | custom-call | flops 917504000 | tf_op jit(solution)/shard_map/far_ahead/pallas_call | solution.py:335
  9.6 0.0 collective-permute-done.2.refs_2_
  9.6 0.0 copy-start
  9.6 2.1 %collective-permute-start.6 = (f32[24,512]{1,0:T(8,128)S(1)}, f32[24,512]{1,0:T(8,128)S(1)}, u32[]{:S(2)}, u32[]{:S(2)}) collective-permute-start(f32[24,512]{1,0:T(8,128)S(1)} %stack.1), channel_id=1, source_target_pairs={{0,16},{4,20},{8,24},{12,28},{16,0},{20,4},{24,8},{28,12},{1,17},{... | collective-permute-start | bytes 147464 | tf_op jit(solution)/shard_map/ppermute | solution.py:394
  11.7 1.5 %far_after.1.refs_1_ = f32[8,512]{1,0:T(8,128)S(1)} custom-call(f32[8,512]{1,0:T(8,128)S(1)} %get-tuple-element.10.own_ref.refs_0_, f32[8,512]{1,0:T(8,128)S(1)} %far_ahead.1.part_ref.after_ref, f32[8,512]{1,0:T(8,128)S(1)} %collective-permute-done.refs_0_, f32[8,512]{1,0:T(8,128)S(1)} %collective-permute-done.1.refs_1_, ...), custom_call_target="tpu_custom_call" | custom-call | flops 3670016000 | tf_op jit(solution)/shard_map/far_after/pallas_call | solution.py:361
  13.2 0.0 collective-permute-done.3.refs_2_
  13.2 0.0 collective-permute-done.4.refs_3_
  13.2 0.0 collective-permute-done.5.refs_4_
  13.2 0.0 copy-done
  13.2 2.4 %near.1.refs_1_ = f32[8,512]{1,0:T(8,128)S(1)} custom-call(f32[8,512]{1,0:T(8,128)S(1)} %get-tuple-element.10.own_ref.refs_0_, f32[8,512]{1,0:T(8,128)S(1)} %far_after.1.refs_1_, f32[1,8,128]{2,1,0:T(8,128)S(1)} %collective-permute-done.3.refs_2_, f32[1,8,128]{2,1,0:T(8,128)S(1)} %collective-permute-done.4.refs_3_, ...), custom_call_target="tpu_custom_call" | custom-call | flops 2752512000 | tf_op jit(solution)/shard_map/near/pallas_call | solution.py:223
  15.6 0.0 collective-permute-done.6.refs_2_
  15.6 3.5 %far_last.1 = f32[3,512]{1,0:T(4,128)} custom-call(f32[8,512]{1,0:T(8,128)S(1)} %get-tuple-element.10.own_ref.refs_0_, f32[8,512]{1,0:T(8,128)S(1)} %near.1.refs_1_, f32[24,512]{1,0:T(8,128)S(1)} %collective-permute-done.6.refs_2_), custom_call_target="tpu_custom_call" | custom-call | flops 2752512000 | tf_op jit(solution)/shard_map/far_last/pallas_call | solution.py:223
  (4 shorter events, 0.0 us)
Async XLA Ops:
  1.6 3.8 %copy-start.1 = (s32[1,12,2]{1,2,0:T(2,128)S(1)}, s32[1,12,2]{1,2,0:T(2,128)}, u32[]{:S(2)}) copy-start(s32[1,12,2]{1,2,0:T(2,128)} %param.9) | copy-start | bytes 292
  1.6 3.8 %copy-start.2 = (s32[1,4]{1,0:T(1,128)S(1)}, s32[1,4]{1,0:T(1,128)}, u32[]{:S(2)}) copy-start(s32[1,4]{1,0:T(1,128)} %map_ref.1) | copy-start | bytes 52
  1.6 6.6 %collective-permute-start = (f32[8,512]{1,0:T(8,128)S(1)}, f32[8,512]{1,0:T(8,128)S(1)}, u32[]{:S(2)}, u32[]{:S(2)}) collective-permute-start(f32[8,512]{1,0:T(8,128)S(1)} %get-tuple-element.10.own_ref.refs_0_), channel_id=1, source_target_pairs={{0,8},{4,12},{8,0},{12,4},{16,24},{20,28},{24,16},{28,20},{1,9},{5... | collective-permute-start | bytes 49160 | tf_op jit(solution)/shard_map/ppermute | solution.py:385
  3.9 4.6 %collective-permute-start.1 = (f32[8,512]{1,0:T(8,128)S(1)}, f32[8,512]{1,0:T(8,128)S(1)}, u32[]{:S(2)}, u32[]{:S(2)}) collective-permute-start(f32[8,512]{1,0:T(8,128)S(1)} %get-tuple-element.10.own_ref.refs_0_), channel_id=1, source_target_pairs={{0,12},{4,8},{8,4},{12,0},{16,28},{20,24},{24,20},{28,16},{1,13},{... | collective-permute-start | bytes 49160 | tf_op jit(solution)/shard_map/ppermute | solution.py:385
  5.3 4.3 %collective-permute-start.2 = (f32[8,512]{1,0:T(8,128)S(1)}, f32[8,512]{1,0:T(8,128)S(1)}, u32[]{:S(2)}, u32[]{:S(2)}) collective-permute-start(f32[8,512]{1,0:T(8,128)S(1)} %get-tuple-element.10.own_ref.refs_0_), channel_id=1, source_target_pairs={{0,4},{4,0},{8,12},{12,8},{16,20},{20,16},{24,28},{28,24},{1,5},{5... | collective-permute-start | bytes 49160 | tf_op jit(solution)/shard_map/ppermute | solution.py:385
  6.2 7.0 %collective-permute-start.3 = (f32[1,8,128]{2,1,0:T(8,128)S(1)}, f32[1,8,128]{2,1,0:T(8,128)S(1)}, u32[]{:S(2)}, u32[]{:S(2)}) collective-permute-start(f32[1,8,128]{2,1,0:T(8,128)S(1)} %get-tuple-element.12), channel_id=1, source_target_pairs={{0,1},{1,0},{2,3},{3,2},{4,5},{5,4},{6,7},{7,6},{8,9},{9,8},{10,11... | collective-permute-start | bytes 12296 | tf_op jit(solution)/shard_map/ppermute | solution.py:387
  6.3 6.9 %collective-permute-start.4 = (f32[1,8,128]{2,1,0:T(8,128)S(1)}, f32[1,8,128]{2,1,0:T(8,128)S(1)}, u32[]{:S(2)}, u32[]{:S(2)}) collective-permute-start(f32[1,8,128]{2,1,0:T(8,128)S(1)} %get-tuple-element.13), channel_id=1, source_target_pairs={{0,2},{1,3},{2,0},{3,1},{4,6},{5,7},{6,4},{7,5},{8,10},{9,11},{10,... | collective-permute-start | bytes 12296 | tf_op jit(solution)/shard_map/ppermute | solution.py:387
  8.2 5.0 %collective-permute-start.5 = (f32[1,8,128]{2,1,0:T(8,128)S(1)}, f32[1,8,128]{2,1,0:T(8,128)S(1)}, u32[]{:S(2)}, u32[]{:S(2)}) collective-permute-start(f32[1,8,128]{2,1,0:T(8,128)S(1)} %get-tuple-element.14), channel_id=1, source_target_pairs={{0,3},{1,2},{2,1},{3,0},{4,7},{5,6},{6,5},{7,4},{8,11},{9,10},{10,... | collective-permute-start | bytes 12296 | tf_op jit(solution)/shard_map/ppermute | solution.py:387
  9.6 3.6 %copy-start = (f32[32,128]{1,0:T(8,128)S(1)}, f32[32,128]{1,0:T(8,128)}, u32[]{:S(2)}) copy-start(f32[32,128]{1,0:T(8,128)} %refs_5_.1) | copy-start | bytes 49156
  9.6 6.0 %collective-permute-start.6 = (f32[24,512]{1,0:T(8,128)S(1)}, f32[24,512]{1,0:T(8,128)S(1)}, u32[]{:S(2)}, u32[]{:S(2)}) collective-permute-start(f32[24,512]{1,0:T(8,128)S(1)} %stack.1), channel_id=1, source_target_pairs={{0,16},{4,20},{8,24},{12,28},{16,0},{20,4},{24,8},{28,12},{1,17},{... | collective-permute-start | bytes 147464 | tf_op jit(solution)/shard_map/ppermute | solution.py:394
